TPU v7x, 512 devices: a whole 4x8x8 slice. The times are simulated.
512 devices in a mesh: row: 8 (over y), col: 32 (over z, x), layer: 2 (over core).
Axes of the slice: x: 4, y: 8, z: 8, core: 2. Of those that a mesh axis runs over, the one named last changes fastest.
Arguments:
- s_values: bfloat16 [8, 32, 2, 128, 128], P('row', 'col'), may hold values from -0.5 to 0.5
- s_slots: int32 [8, 32, 2], P('row', 'col'), may hold values from 0 to 16, as said below
- x_values: bfloat16 [4, 8, 32, 1, 128, 128], P(None, 'row', 'col'), may hold values from -6 to 6
- x_slots: int32 [4, 8, 32, 1], P(None, 'row', 'col'), may hold values from 0 to 3, as said below
Outputs:
- product: float32 [8192, 8192], P(('row', 'layer'), 'col')
Inputs may be any that keep to these rules, and one draw needn't show every extreme that they name: `s_slots`: within one piece the live values are distinct; the value 8 * 2 marks an empty slot, empty slots follow the live ones, every piece has at least one live slot, and at least one piece has all 2 slots live. `x_slots`: within one piece the 1 positions are distinct.
All inputs are finite; a program needn't handle non-finite values.
Results may differ from a plain program's by a relative error of at most 0.0003.
Values may be sent and summed in bfloat16 or wider, within the bound.
A program may use at most 64 MiB of HBM per device.

v0:
```python
import jax
import jax.numpy as jnp
from jax import lax
from jax.sharding import PartitionSpec as P

BR = 8
BC = 2


def for_sending(value):

    def short(part):
        return part.astype(jnp.bfloat16) if part.dtype == jnp.float32 else part

    return jax.tree.map(short, value)


def passed_along(value, axis, by):
    count = lax.axis_size(axis)
    return lax.ppermute(value, axis, [(i, (i + by) % count) for i in range(count)])


def bit_count(value):
    return value.bit_length()


def align(held, amount, width, levels, axis_kind):
    for level in range(levels):
        distance = (1 << level) % width
        if axis_kind == "col_full":
            moved = jax.tree.map(
                lambda part, own: part.astype(own.dtype),
                passed_along(for_sending(held), "col", width - distance),
                held,
            )
        else:
            moved = jax.tree.map(
                lambda part, own: part.astype(own.dtype),
                passed_along(for_sending(held), "row", width - distance),
                held,
            )
        taken = amount >> level & 1 == 1
        held = jax.tree.map(lambda fresh, stale: jnp.where(taken, fresh, stale), moved, held)
    return held


def expand_density(piece_values, piece_slots, inner, block):
    kx_count = piece_slots.shape[0]
    columns = BC
    one_hot = (
        piece_slots[None, :] == jnp.arange(inner * columns, dtype=jnp.int32)[:, None]
    ).astype(jnp.bfloat16)
    flat = jnp.dot(
        one_hot, piece_values.reshape(kx_count, block * block), preferred_element_type=jnp.float32
    )
    tiles = flat.astype(jnp.bfloat16).reshape(inner, columns, block, block)
    return tiles.transpose(0, 2, 1, 3).reshape(inner * block, columns * block)


def dense_kernel(total, s_piece, s_pos, x_tile, inner, block):
    ks_count = s_pos.shape[0]
    one_hot = (s_pos[None, :] == jnp.arange(BR * inner, dtype=jnp.int32)[:, None]).astype(
        jnp.bfloat16
    )
    flat = jnp.dot(
        one_hot, s_piece.reshape(ks_count, block * block), preferred_element_type=jnp.float32
    )
    tiles = flat.astype(jnp.bfloat16).reshape(BR, inner, block, block)
    s_tile = tiles.transpose(0, 2, 1, 3).reshape(BR * block, inner * block)
    return total + jnp.dot(s_tile, x_tile, preferred_element_type=jnp.float32)


def per_device(s_values, s_slots, x_values, x_slots):
    n_row = lax.axis_size("row")
    n_col = lax.axis_size("col")
    n_layer = lax.axis_size("layer")
    row_id = lax.axis_index("row")
    col_id = lax.axis_index("col")
    layer_id = lax.axis_index("layer")
    per_layer = n_col // n_layer
    inner = n_row * BR // n_col
    block = s_values.shape[-1]
    held_s = (s_values[0, 0], s_slots[0, 0])
    s_offset = row_id + layer_id * per_layer
    held_s = align(held_s, s_offset % n_col, n_col, bit_count(n_col - 1), "col_full")
    shift_x = (col_id + layer_id * per_layer) % n_row
    held_x = align(
        (x_values[:, 0, 0], x_slots[:, 0, 0]), shift_x, n_row, bit_count(n_row - 1), "row_full"
    )
    start_piece = col_id + row_id + layer_id * per_layer
    total = jnp.zeros((BR * block, BC * block), jnp.float32)
    for turn in range(per_layer):
        piece = (start_piece + turn) % n_col
        group_pick = piece // n_row
        piece_values = lax.dynamic_index_in_dim(held_x[0], group_pick, 0, keepdims=False)
        piece_slots = lax.dynamic_index_in_dim(held_x[1], group_pick, 0, keepdims=False)
        x_tile = expand_density(piece_values, piece_slots, inner, block)
        total = dense_kernel(total, held_s[0], held_s[1], x_tile, inner, block)
        if turn + 1 < per_layer:
            held_s = jax.tree.map(
                lambda part, own: part.astype(own.dtype),
                passed_along(for_sending(held_s), "col", n_col - 1),
                held_s,
            )
            held_x = jax.tree.map(
                lambda part, own: part.astype(own.dtype),
                passed_along(for_sending(held_x), "row", n_row - 1),
                held_x,
            )
    return lax.psum_scatter(total, "layer", scatter_dimension=0, tiled=True)


def solution(mesh):
    placed = (
        P("row", "col", None, None, None),
        P("row", "col", None),
        P(None, "row", "col", None, None, None),
        P(None, "row", "col", None),
    )
    return jax.shard_map(
        per_device,
        mesh=mesh,
        in_specs=placed,
        out_specs=P(("row", "layer"), "col"),
        check_vma=False,
    )
```

profile of v0, /device:TPU:1, one launch (start us, length us, event | category | flops | bytes accessed | tf_op | source)
XLA Modules:
  0.0 516.0 jit_solution(13884088623409240374)
XLA Ops:
  6.5 13.8 %collective-permute-start.5 = (bf16[2,128,128]{2,1,0:T(8,128)(2,1)}, bf16[2,128,128]{2,1,0:T(8,128)(2,1)S(1)}, u32[]{:S(2)}, u32[]{:S(2)}) collective-permute-start(bf16[2,128,128]{2,1,0:T(8,128)(2,1)} %bitcast.602), channel_id=1, source_target_pairs={{0,62},{2,0},{4,2},{6,4},{8,6},{10,8},{12,10},{14,12},{16,14},{18,... | collective-permute-start | bytes 196616 | tf_op jit(solution)/shard_map/ppermute | solution.py:20
  22.8 5.1 collective-permute-start.13
  56.7 5.3 %collective-permute-start.16 = (s32[2]{0:T(128)S(1)}, s32[2]{0:T(128)S(1)}, u32[]{:S(2)}, u32[]{:S(2)}) collective-permute-start(s32[2]{0:T(128)S(1)} %broadcast_select_fusion.15), channel_id=1, source_target_pairs={{0,62},{2,0},{4,2},{6,4},{8,6},{10,8},{12,10},{14,12},{16,14},{18,... | collective-permute-start | bytes 32 | tf_op jit(solution)/shard_map/ppermute | solution.py:20
  70.3 6.9 %collective-permute-start.24 = (s32[2]{0:T(128)S(1)}, s32[2]{0:T(128)S(1)}, u32[]{:S(2)}, u32[]{:S(2)}) collective-permute-start(s32[2]{0:T(128)S(1)} %collective-permute-done.20), channel_id=1, source_target_pairs={{0,62},{2,0},{4,2},{6,4},{8,6},{10,8},{12,10},{14,12},{16,14},{18,... | collective-permute-start | bytes 32 | tf_op jit(solution)/shard_map/ppermute | solution.py:20
  85.5 6.9 %collective-permute-start.32 = (s32[2]{0:T(128)S(1)}, s32[2]{0:T(128)S(1)}, u32[]{:S(2)}, u32[]{:S(2)}) collective-permute-start(s32[2]{0:T(128)S(1)} %collective-permute-done.28), channel_id=1, source_target_pairs={{0,62},{2,0},{4,2},{6,4},{8,6},{10,8},{12,10},{14,12},{16,14},{18,... | collective-permute-start | bytes 32 | tf_op jit(solution)/shard_map/ppermute | solution.py:20
  93.1 6.9 %collective-permute-start.36 = (s32[2]{0:T(128)S(1)}, s32[2]{0:T(128)S(1)}, u32[]{:S(2)}, u32[]{:S(2)}) collective-permute-start(s32[2]{0:T(128)S(1)} %collective-permute-done.32), channel_id=1, source_target_pairs={{0,62},{2,0},{4,2},{6,4},{8,6},{10,8},{12,10},{14,12},{16,14},{18,... | collective-permute-start | bytes 32 | tf_op jit(solution)/shard_map/ppermute | solution.py:20
  108.9 6.3 %collective-permute-start.44 = (s32[2]{0:T(128)S(1)}, s32[2]{0:T(128)S(1)}, u32[]{:S(2)}, u32[]{:S(2)}) collective-permute-start(s32[2]{0:T(128)S(1)} %collective-permute-done.40), channel_id=1, source_target_pairs={{0,62},{2,0},{4,2},{6,4},{8,6},{10,8},{12,10},{14,12},{16,14},{18,... | collective-permute-start | bytes 32 | tf_op jit(solution)/shard_map/ppermute | solution.py:20
  124.1 6.3 %collective-permute-start.52 = (s32[2]{0:T(128)S(1)}, s32[2]{0:T(128)S(1)}, u32[]{:S(2)}, u32[]{:S(2)}) collective-permute-start(s32[2]{0:T(128)S(1)} %collective-permute-done.48), channel_id=1, source_target_pairs={{0,62},{2,0},{4,2},{6,4},{8,6},{10,8},{12,10},{14,12},{16,14},{18,... | collective-permute-start | bytes 32 | tf_op jit(solution)/shard_map/ppermute | solution.py:20
  146.8 6.3 %collective-permute-start.64 = (s32[2]{0:T(128)S(1)}, s32[2]{0:T(128)S(1)}, u32[]{:S(2)}, u32[]{:S(2)}) collective-permute-start(s32[2]{0:T(128)S(1)} %collective-permute-done.60), channel_id=1, source_target_pairs={{0,62},{2,0},{4,2},{6,4},{8,6},{10,8},{12,10},{14,12},{16,14},{18,... | collective-permute-start | bytes 32 | tf_op jit(solution)/shard_map/ppermute | solution.py:20
  162.1 6.4 %collective-permute-start.72 = (s32[2]{0:T(128)}, s32[2]{0:T(128)}, u32[]{:S(2)}, u32[]{:S(2)}) collective-permute-start(s32[2]{0:T(128)} %collective-permute-done.68), channel_id=1, source_target_pairs={{0,62},{2,0},{4,2},{6,4},{8,6},{10,8},{12,10},{14,12},{16,14},{18,... | collective-permute-start | bytes 32 | tf_op jit(solution)/shard_map/ppermute | solution.py:20
  238.5 5.7 %collective-permute-start.9 = (bf16[2,128,128]{2,1,0:T(8,128)(2,1)S(1)}, bf16[2,128,128]{2,1,0:T(8,128)(2,1)S(1)}, u32[]{:S(2)}, u32[]{:S(2)}) collective-permute-start(bf16[2,128,128]{2,1,0:T(8,128)(2,1)S(1)} %broadcast_select_fusion.6), channel_id=1, source_target_pairs={{0,32},{2,34},{4,36},{6,38},{8,40},{10,42},{12,44},{14,46},{16,48}... | collective-permute-start | bytes 196616 | tf_op jit(solution)/shard_map/ppermute | solution.py:20
  248.5 6.2 %collective-permute-start.17 = (bf16[2,128,128]{2,1,0:T(8,128)(2,1)S(1)}, bf16[2,128,128]{2,1,0:T(8,128)(2,1)S(1)}, u32[]{:S(2)}, u32[]{:S(2)}) collective-permute-start(bf16[2,128,128]{2,1,0:T(8,128)(2,1)S(1)} %broadcast_select_fusion.7), channel_id=1, source_target_pairs={{0,62},{2,0},{4,2},{6,4},{8,6},{10,8},{12,10},{14,12},{16,14},{18,... | collective-permute-start | bytes 196616 | tf_op jit(solution)/shard_map/ppermute | solution.py:20
  258.0 5.8 %collective-permute-start.21 = (bf16[2,128,128]{2,1,0:T(8,128)(2,1)S(1)}, bf16[2,128,128]{2,1,0:T(8,128)(2,1)S(1)}, u32[]{:S(2)}, u32[]{:S(2)}) collective-permute-start(bf16[2,128,128]{2,1,0:T(8,128)(2,1)S(1)} %collective-permute-done.17), channel_id=1, source_target_pairs={{0,62},{2,0},{4,2},{6,4},{8,6},{10,8},{12,10},{14,12},{16,14},{18,... | collective-permute-start | bytes 196616 | tf_op jit(solution)/shard_map/ppermute | solution.py:20
  265.8 7.0 %collective-permute-start.25 = (bf16[2,128,128]{2,1,0:T(8,128)(2,1)S(1)}, bf16[2,128,128]{2,1,0:T(8,128)(2,1)S(1)}, u32[]{:S(2)}, u32[]{:S(2)}) collective-permute-start(bf16[2,128,128]{2,1,0:T(8,128)(2,1)S(1)} %collective-permute-done.21), channel_id=1, source_target_pairs={{0,62},{2,0},{4,2},{6,4},{8,6},{10,8},{12,10},{14,12},{16,14},{18,... | collective-permute-start | bytes 196616 | tf_op jit(solution)/shard_map/ppermute | solution.py:20
  274.1 7.0 %collective-permute-start.29 = (bf16[2,128,128]{2,1,0:T(8,128)(2,1)S(1)}, bf16[2,128,128]{2,1,0:T(8,128)(2,1)S(1)}, u32[]{:S(2)}, u32[]{:S(2)}) collective-permute-start(bf16[2,128,128]{2,1,0:T(8,128)(2,1)S(1)} %collective-permute-done.25), channel_id=1, source_target_pairs={{0,62},{2,0},{4,2},{6,4},{8,6},{10,8},{12,10},{14,12},{16,14},{18,... | collective-permute-start | bytes 196616 | tf_op jit(solution)/shard_map/ppermute | solution.py:20
  283.8 5.8 %collective-permute-start.33 = (bf16[2,128,128]{2,1,0:T(8,128)(2,1)S(1)}, bf16[2,128,128]{2,1,0:T(8,128)(2,1)S(1)}, u32[]{:S(2)}, u32[]{:S(2)}) collective-permute-start(bf16[2,128,128]{2,1,0:T(8,128)(2,1)S(1)} %collective-permute-done.29), channel_id=1, source_target_pairs={{0,62},{2,0},{4,2},{6,4},{8,6},{10,8},{12,10},{14,12},{16,14},{18,... | collective-permute-start | bytes 196616 | tf_op jit(solution)/shard_map/ppermute | solution.py:20
  293.2 6.5 %collective-permute-start.37 = (bf16[2,128,128]{2,1,0:T(8,128)(2,1)S(1)}, bf16[2,128,128]{2,1,0:T(8,128)(2,1)S(1)}, u32[]{:S(2)}, u32[]{:S(2)}) collective-permute-start(bf16[2,128,128]{2,1,0:T(8,128)(2,1)S(1)} %collective-permute-done.33), channel_id=1, source_target_pairs={{0,62},{2,0},{4,2},{6,4},{8,6},{10,8},{12,10},{14,12},{16,14},{18,... | collective-permute-start | bytes 196616 | tf_op jit(solution)/shard_map/ppermute | solution.py:20
  302.3 5.7 %collective-permute-start.41 = (bf16[2,128,128]{2,1,0:T(8,128)(2,1)S(1)}, bf16[2,128,128]{2,1,0:T(8,128)(2,1)S(1)}, u32[]{:S(2)}, u32[]{:S(2)}) collective-permute-start(bf16[2,128,128]{2,1,0:T(8,128)(2,1)S(1)} %collective-permute-done.37), channel_id=1, source_target_pairs={{0,62},{2,0},{4,2},{6,4},{8,6},{10,8},{12,10},{14,12},{16,14},{18,... | collective-permute-start | bytes 196616 | tf_op jit(solution)/shard_map/ppermute | solution.py:20
  311.5 6.6 %collective-permute-start.45 = (bf16[2,128,128]{2,1,0:T(8,128)(2,1)S(1)}, bf16[2,128,128]{2,1,0:T(8,128)(2,1)S(1)}, u32[]{:S(2)}, u32[]{:S(2)}) collective-permute-start(bf16[2,128,128]{2,1,0:T(8,128)(2,1)S(1)} %collective-permute-done.41), channel_id=1, source_target_pairs={{0,62},{2,0},{4,2},{6,4},{8,6},{10,8},{12,10},{14,12},{16,14},{18,... | collective-permute-start | bytes 196616 | tf_op jit(solution)/shard_map/ppermute | solution.py:20
  321.0 5.8 %collective-permute-start.49 = (bf16[2,128,128]{2,1,0:T(8,128)(2,1)S(1)}, bf16[2,128,128]{2,1,0:T(8,128)(2,1)S(1)}, u32[]{:S(2)}, u32[]{:S(2)}) collective-permute-start(bf16[2,128,128]{2,1,0:T(8,128)(2,1)S(1)} %collective-permute-done.45), channel_id=1, source_target_pairs={{0,62},{2,0},{4,2},{6,4},{8,6},{10,8},{12,10},{14,12},{16,14},{18,... | collective-permute-start | bytes 196616 | tf_op jit(solution)/shard_map/ppermute | solution.py:20
  330.4 6.3 %collective-permute-start.53 = (bf16[2,128,128]{2,1,0:T(8,128)(2,1)S(1)}, bf16[2,128,128]{2,1,0:T(8,128)(2,1)S(1)}, u32[]{:S(2)}, u32[]{:S(2)}) collective-permute-start(bf16[2,128,128]{2,1,0:T(8,128)(2,1)S(1)} %collective-permute-done.49), channel_id=1, source_target_pairs={{0,62},{2,0},{4,2},{6,4},{8,6},{10,8},{12,10},{14,12},{16,14},{18,... | collective-permute-start | bytes 196616 | tf_op jit(solution)/shard_map/ppermute | solution.py:20
  341.9 4.8 collective-permute-start.57
  349.7 5.2 %collective-permute-start.61 = (bf16[2,128,128]{2,1,0:T(8,128)(2,1)S(1)}, bf16[2,128,128]{2,1,0:T(8,128)(2,1)S(1)}, u32[]{:S(2)}, u32[]{:S(2)}) collective-permute-start(bf16[2,128,128]{2,1,0:T(8,128)(2,1)S(1)} %collective-permute-done.57), channel_id=1, source_target_pairs={{0,62},{2,0},{4,2},{6,4},{8,6},{10,8},{12,10},{14,12},{16,14},{18,... | collective-permute-start | bytes 196616 | tf_op jit(solution)/shard_map/ppermute | solution.py:20
  357.9 6.3 %collective-permute-start.65 = (bf16[2,128,128]{2,1,0:T(8,128)(2,1)S(1)}, bf16[2,128,128]{2,1,0:T(8,128)(2,1)S(1)}, u32[]{:S(2)}, u32[]{:S(2)}) collective-permute-start(bf16[2,128,128]{2,1,0:T(8,128)(2,1)S(1)} %collective-permute-done.61), channel_id=1, source_target_pairs={{0,62},{2,0},{4,2},{6,4},{8,6},{10,8},{12,10},{14,12},{16,14},{18,... | collective-permute-start | bytes 196616 | tf_op jit(solution)/shard_map/ppermute | solution.py:20
  367.2 5.3 %collective-permute-start.69 = (bf16[2,128,128]{2,1,0:T(8,128)(2,1)S(1)}, bf16[2,128,128]{2,1,0:T(8,128)(2,1)S(1)}, u32[]{:S(2)}, u32[]{:S(2)}) collective-permute-start(bf16[2,128,128]{2,1,0:T(8,128)(2,1)S(1)} %collective-permute-done.65), channel_id=1, source_target_pairs={{0,62},{2,0},{4,2},{6,4},{8,6},{10,8},{12,10},{14,12},{16,14},{18,... | collective-permute-start | bytes 196616 | tf_op jit(solution)/shard_map/ppermute | solution.py:20
  375.3 7.0 %collective-permute-start.73 = (bf16[2,128,128]{2,1,0:T(8,128)(2,1)S(1)}, bf16[2,128,128]{2,1,0:T(8,128)(2,1)S(1)}, u32[]{:S(2)}, u32[]{:S(2)}) collective-permute-start(bf16[2,128,128]{2,1,0:T(8,128)(2,1)S(1)} %collective-permute-done.69), channel_id=1, source_target_pairs={{0,62},{2,0},{4,2},{6,4},{8,6},{10,8},{12,10},{14,12},{16,14},{18,... | collective-permute-start | bytes 196616 | tf_op jit(solution)/shard_map/ppermute | solution.py:20
  401.7 5.0 collective-permute-start.59
  408.9 5.0 collective-permute-start.63
  417.4 5.3 %collective-permute-start.67 = (bf16[4,1,128,128]{3,2,0,1:T(8,128)(2,1)S(1)}, bf16[4,1,128,128]{3,2,0,1:T(8,128)(2,1)S(1)}, u32[]{:S(2)}, u32[]{:S(2)}) collective-permute-start(bf16[4,1,128,128]{3,2,0,1:T(8,128)(2,1)S(1)} %collective-permute-done.63), channel_id=1, source_target_pairs={{0,448},{64,0},{128,64},{192,128},{256,192},{320,256},{384,320},{4... | collective-permute-start | bytes 393224 | tf_op jit(solution)/shard_map/ppermute | solution.py:20
  424.9 5.0 collective-permute-start.71
  432.1 5.0 collective-permute-start.75
  441.1 68.0 %reduce-scatter.2.cloned.1.call-done = f32[512,256]{1,0:T(8,128)} async-done(((f32[1024,256]{1,0:T(8,128)}), f32[512,256]{1,0:T(8,128)}) %reduce-scatter.2.cloned.1.call-update) | async-done | bytes 524304 | tf_op jit(solution)/shard_map/reduce_scatter | solution.py:110
  (385 shorter events, 239.2 us)
Async XLA Ops:
  6.5 502.7 %reduce-scatter.2.cloned.1.call-start = ((), (), s32[]{:S(2)}) async-start(), calls=%async_computation.1 | async-start | bytes 1572864 | tf_op jit(solution)/shard_map/reduce_scatter | solution.py:110
  6.5 213.7 %collective-permute-start.5 = (bf16[2,128,128]{2,1,0:T(8,128)(2,1)}, bf16[2,128,128]{2,1,0:T(8,128)(2,1)S(1)}, u32[]{:S(2)}, u32[]{:S(2)}) collective-permute-start(bf16[2,128,128]{2,1,0:T(8,128)(2,1)} %bitcast.602), channel_id=1, source_target_pairs={{0,62},{2,0},{4,2},{6,4},{8,6},{10,8},{12,10},{14,12},{16,14},{18,... | collective-permute-start | bytes 196616 | tf_op jit(solution)/shard_map/ppermute | solution.py:20
  20.4 11.2 %collective-permute-start = (s32[2]{0:T(128)S(1)}, s32[2]{0:T(128)S(1)}, u32[]{:S(2)}, u32[]{:S(2)}) collective-permute-start(s32[2]{0:T(128)S(1)} %bitcast.618), channel_id=1, source_target_pairs={{0,62},{2,0},{4,2},{6,4},{8,6},{10,8},{12,10},{14,12},{16,14},{18,... | collective-permute-start | bytes 32 | tf_op jit(solution)/shard_map/ppermute | solution.py:20
  22.8 211.0 %collective-permute-start.13 = (bf16[4,1,128,128]{3,2,0,1:T(8,128)(2,1)}, bf16[4,1,128,128]{3,2,0,1:T(8,128)(2,1)S(1)}, u32[]{:S(2)}, u32[]{:S(2)}) collective-permute-start(bf16[4,1,128,128]{3,2,0,1:T(8,128)(2,1)} %bitcast.601), channel_id=1, source_target_pairs={{0,448},{64,0},{128,64},{192,128},{256,192},{320,256},{384,320},{4... | collective-permute-start | bytes 393224 | tf_op jit(solution)/shard_map/ppermute | solution.py:20
  28.0 11.6 %collective-permute-start.10 = (s32[4,1]{0,1:T(1,128)S(1)}, s32[4,1]{0,1:T(1,128)S(1)}, u32[]{:S(2)}, u32[]{:S(2)}) collective-permute-start(s32[4,1]{0,1:T(1,128)S(1)} %bitcast.619), channel_id=1, source_target_pairs={{0,448},{64,0},{128,64},{192,128},{256,192},{320,256},{384,320},{4... | collective-permute-start | bytes 56 | tf_op jit(solution)/shard_map/ppermute | solution.py:20
  39.6 10.9 %collective-permute-start.11 = (s32[4,1]{0,1:T(1,128)S(1)}, s32[4,1]{0,1:T(1,128)S(1)}, u32[]{:S(2)}, u32[]{:S(2)}) collective-permute-start(s32[4,1]{0,1:T(1,128)S(1)} %broadcast_select_fusion.8), channel_id=1, source_target_pairs={{0,384},{64,448},{128,0},{192,64},{256,128},{320,192},{384,256},{4... | collective-permute-start | bytes 56 | tf_op jit(solution)/shard_map/ppermute | solution.py:20
  50.5 11.6 %collective-permute-start.12 = (s32[4,1]{0,1:T(1,128)S(1)}, s32[4,1]{0,1:T(1,128)S(1)}, u32[]{:S(2)}, u32[]{:S(2)}) collective-permute-start(s32[4,1]{0,1:T(1,128)S(1)} %broadcast_select_fusion.9), channel_id=1, source_target_pairs={{0,256},{64,320},{128,384},{192,448},{256,0},{320,64},{384,128},{4... | collective-permute-start | bytes 56 | tf_op jit(solution)/shard_map/ppermute | solution.py:20
  62.1 15.2 %collective-permute-start.18 = (s32[4,1]{0,1:T(1,128)S(1)}, s32[4,1]{0,1:T(1,128)S(1)}, u32[]{:S(2)}, u32[]{:S(2)}) collective-permute-start(s32[4,1]{0,1:T(1,128)S(1)} %broadcast_select_fusion.10), channel_id=1, source_target_pairs={{0,448},{64,0},{128,64},{192,128},{256,192},{320,256},{384,320},{4... | collective-permute-start | bytes 56 | tf_op jit(solution)/shard_map/ppermute | solution.py:20
  70.3 10.9 %collective-permute-start.24 = (s32[2]{0:T(128)S(1)}, s32[2]{0:T(128)S(1)}, u32[]{:S(2)}, u32[]{:S(2)}) collective-permute-start(s32[2]{0:T(128)S(1)} %collective-permute-done.20), channel_id=1, source_target_pairs={{0,62},{2,0},{4,2},{6,4},{8,6},{10,8},{12,10},{14,12},{16,14},{18,... | collective-permute-start | bytes 32 | tf_op jit(solution)/shard_map/ppermute | solution.py:20
  78.5 21.5 %collective-permute-start.22 = (s32[4,1]{0,1:T(1,128)S(1)}, s32[4,1]{0,1:T(1,128)S(1)}, u32[]{:S(2)}, u32[]{:S(2)}) collective-permute-start(s32[4,1]{0,1:T(1,128)S(1)} %collective-permute-done.18), channel_id=1, source_target_pairs={{0,448},{64,0},{128,64},{192,128},{256,192},{320,256},{384,320},{4... | collective-permute-start | bytes 56 | tf_op jit(solution)/shard_map/ppermute | solution.py:20
  93.1 11.4 %collective-permute-start.36 = (s32[2]{0:T(128)S(1)}, s32[2]{0:T(128)S(1)}, u32[]{:S(2)}, u32[]{:S(2)}) collective-permute-start(s32[2]{0:T(128)S(1)} %collective-permute-done.32), channel_id=1, source_target_pairs={{0,62},{2,0},{4,2},{6,4},{8,6},{10,8},{12,10},{14,12},{16,14},{18,... | collective-permute-start | bytes 32 | tf_op jit(solution)/shard_map/ppermute | solution.py:20
  101.8 13.4 %collective-permute-start.26 = (s32[4,1]{0,1:T(1,128)S(1)}, s32[4,1]{0,1:T(1,128)S(1)}, u32[]{:S(2)}, u32[]{:S(2)}) collective-permute-start(s32[4,1]{0,1:T(1,128)S(1)} %collective-permute-done.22), channel_id=1, source_target_pairs={{0,448},{64,0},{128,64},{192,128},{256,192},{320,256},{384,320},{4... | collective-permute-start | bytes 56 | tf_op jit(solution)/shard_map/ppermute | solution.py:20
  108.9 10.9 %collective-permute-start.44 = (s32[2]{0:T(128)S(1)}, s32[2]{0:T(128)S(1)}, u32[]{:S(2)}, u32[]{:S(2)}) collective-permute-start(s32[2]{0:T(128)S(1)} %collective-permute-done.40), channel_id=1, source_target_pairs={{0,62},{2,0},{4,2},{6,4},{8,6},{10,8},{12,10},{14,12},{16,14},{18,... | collective-permute-start | bytes 32 | tf_op jit(solution)/shard_map/ppermute | solution.py:20
  117.1 13.4 %collective-permute-start.30 = (s32[4,1]{0,1:T(1,128)S(1)}, s32[4,1]{0,1:T(1,128)S(1)}, u32[]{:S(2)}, u32[]{:S(2)}) collective-permute-start(s32[4,1]{0,1:T(1,128)S(1)} %collective-permute-done.26), channel_id=1, source_target_pairs={{0,448},{64,0},{128,64},{192,128},{256,192},{320,256},{384,320},{4... | collective-permute-start | bytes 56 | tf_op jit(solution)/shard_map/ppermute | solution.py:20
  124.1 10.8 %collective-permute-start.52 = (s32[2]{0:T(128)S(1)}, s32[2]{0:T(128)S(1)}, u32[]{:S(2)}, u32[]{:S(2)}) collective-permute-start(s32[2]{0:T(128)S(1)} %collective-permute-done.48), channel_id=1, source_target_pairs={{0,62},{2,0},{4,2},{6,4},{8,6},{10,8},{12,10},{14,12},{16,14},{18,... | collective-permute-start | bytes 32 | tf_op jit(solution)/shard_map/ppermute | solution.py:20
  139.8 13.4 %collective-permute-start.38 = (s32[4,1]{0,1:T(1,128)S(1)}, s32[4,1]{0,1:T(1,128)S(1)}, u32[]{:S(2)}, u32[]{:S(2)}) collective-permute-start(s32[4,1]{0,1:T(1,128)S(1)} %collective-permute-done.34), channel_id=1, source_target_pairs={{0,448},{64,0},{128,64},{192,128},{256,192},{320,256},{384,320},{4... | collective-permute-start | bytes 56 | tf_op jit(solution)/shard_map/ppermute | solution.py:20
  146.8 10.8 %collective-permute-start.64 = (s32[2]{0:T(128)S(1)}, s32[2]{0:T(128)S(1)}, u32[]{:S(2)}, u32[]{:S(2)}) collective-permute-start(s32[2]{0:T(128)S(1)} %collective-permute-done.60), channel_id=1, source_target_pairs={{0,62},{2,0},{4,2},{6,4},{8,6},{10,8},{12,10},{14,12},{16,14},{18,... | collective-permute-start | bytes 32 | tf_op jit(solution)/shard_map/ppermute | solution.py:20
  154.9 13.5 %collective-permute-start.42 = (s32[4,1]{0,1:T(1,128)S(1)}, s32[4,1]{0,1:T(1,128)S(1)}, u32[]{:S(2)}, u32[]{:S(2)}) collective-permute-start(s32[4,1]{0,1:T(1,128)S(1)} %collective-permute-done.38), channel_id=1, source_target_pairs={{0,448},{64,0},{128,64},{192,128},{256,192},{320,256},{384,320},{4... | collective-permute-start | bytes 56 | tf_op jit(solution)/shard_map/ppermute | solution.py:20
  162.1 223.3 %collective-permute-start.72 = (s32[2]{0:T(128)}, s32[2]{0:T(128)}, u32[]{:S(2)}, u32[]{:S(2)}) collective-permute-start(s32[2]{0:T(128)} %collective-permute-done.68), channel_id=1, source_target_pairs={{0,62},{2,0},{4,2},{6,4},{8,6},{10,8},{12,10},{14,12},{16,14},{18,... | collective-permute-start | bytes 32 | tf_op jit(solution)/shard_map/ppermute | solution.py:20
  233.9 10.4 %collective-permute-start.14 = (bf16[4,1,128,128]{3,2,0,1:T(8,128)(2,1)S(1)}, bf16[4,1,128,128]{3,2,0,1:T(8,128)(2,1)S(1)}, u32[]{:S(2)}, u32[]{:S(2)}) collective-permute-start(bf16[4,1,128,128]{3,2,0,1:T(8,128)(2,1)S(1)} %broadcast_select_fusion), channel_id=1, source_target_pairs={{0,384},{64,448},{128,0},{192,64},{256,128},{320,192},{384,256},{4... | collective-permute-start | bytes 393224 | tf_op jit(solution)/shard_map/ppermute | solution.py:20
  238.5 9.9 %collective-permute-start.9 = (bf16[2,128,128]{2,1,0:T(8,128)(2,1)S(1)}, bf16[2,128,128]{2,1,0:T(8,128)(2,1)S(1)}, u32[]{:S(2)}, u32[]{:S(2)}) collective-permute-start(bf16[2,128,128]{2,1,0:T(8,128)(2,1)S(1)} %broadcast_select_fusion.6), channel_id=1, source_target_pairs={{0,32},{2,34},{4,36},{6,38},{8,40},{10,42},{12,44},{14,46},{16,48}... | collective-permute-start | bytes 196616 | tf_op jit(solution)/shard_map/ppermute | solution.py:20
  244.3 11.0 %collective-permute-start.15 = (bf16[4,1,128,128]{3,2,0,1:T(8,128)(2,1)S(1)}, bf16[4,1,128,128]{3,2,0,1:T(8,128)(2,1)S(1)}, u32[]{:S(2)}, u32[]{:S(2)}) collective-permute-start(bf16[4,1,128,128]{3,2,0,1:T(8,128)(2,1)S(1)} %broadcast_select_fusion.1), channel_id=1, source_target_pairs={{0,256},{64,320},{128,384},{192,448},{256,0},{320,64},{384,128},{4... | collective-permute-start | bytes 393224 | tf_op jit(solution)/shard_map/ppermute | solution.py:20
  248.5 9.5 %collective-permute-start.17 = (bf16[2,128,128]{2,1,0:T(8,128)(2,1)S(1)}, bf16[2,128,128]{2,1,0:T(8,128)(2,1)S(1)}, u32[]{:S(2)}, u32[]{:S(2)}) collective-permute-start(bf16[2,128,128]{2,1,0:T(8,128)(2,1)S(1)} %broadcast_select_fusion.7), channel_id=1, source_target_pairs={{0,62},{2,0},{4,2},{6,4},{8,6},{10,8},{12,10},{14,12},{16,14},{18,... | collective-permute-start | bytes 196616 | tf_op jit(solution)/shard_map/ppermute | solution.py:20
  255.4 17.4 %collective-permute-start.19 = (bf16[4,1,128,128]{3,2,0,1:T(8,128)(2,1)S(1)}, bf16[4,1,128,128]{3,2,0,1:T(8,128)(2,1)S(1)}, u32[]{:S(2)}, u32[]{:S(2)}) collective-permute-start(bf16[4,1,128,128]{3,2,0,1:T(8,128)(2,1)S(1)} %broadcast_select_fusion.2), channel_id=1, source_target_pairs={{0,448},{64,0},{128,64},{192,128},{256,192},{320,256},{384,320},{4... | collective-permute-start | bytes 393224 | tf_op jit(solution)/shard_map/ppermute | solution.py:20
  274.1 9.6 %collective-permute-start.29 = (bf16[2,128,128]{2,1,0:T(8,128)(2,1)S(1)}, bf16[2,128,128]{2,1,0:T(8,128)(2,1)S(1)}, u32[]{:S(2)}, u32[]{:S(2)}) collective-permute-start(bf16[2,128,128]{2,1,0:T(8,128)(2,1)S(1)} %collective-permute-done.25), channel_id=1, source_target_pairs={{0,62},{2,0},{4,2},{6,4},{8,6},{10,8},{12,10},{14,12},{16,14},{18,... | collective-permute-start | bytes 196616 | tf_op jit(solution)/shard_map/ppermute | solution.py:20
  281.9 17.8 %collective-permute-start.23 = (bf16[4,1,128,128]{3,2,0,1:T(8,128)(2,1)S(1)}, bf16[4,1,128,128]{3,2,0,1:T(8,128)(2,1)S(1)}, u32[]{:S(2)}, u32[]{:S(2)}) collective-permute-start(bf16[4,1,128,128]{3,2,0,1:T(8,128)(2,1)S(1)} %collective-permute-done.19), channel_id=1, source_target_pairs={{0,448},{64,0},{128,64},{192,128},{256,192},{320,256},{384,320},{4... | collective-permute-start | bytes 393224 | tf_op jit(solution)/shard_map/ppermute | solution.py:20
  300.4 17.7 %collective-permute-start.27 = (bf16[4,1,128,128]{3,2,0,1:T(8,128)(2,1)S(1)}, bf16[4,1,128,128]{3,2,0,1:T(8,128)(2,1)S(1)}, u32[]{:S(2)}, u32[]{:S(2)}) collective-permute-start(bf16[4,1,128,128]{3,2,0,1:T(8,128)(2,1)S(1)} %collective-permute-done.23), channel_id=1, source_target_pairs={{0,448},{64,0},{128,64},{192,128},{256,192},{320,256},{384,320},{4... | collective-permute-start | bytes 393224 | tf_op jit(solution)/shard_map/ppermute | solution.py:20
  318.8 17.9 %collective-permute-start.31 = (bf16[4,1,128,128]{3,2,0,1:T(8,128)(2,1)S(1)}, bf16[4,1,128,128]{3,2,0,1:T(8,128)(2,1)S(1)}, u32[]{:S(2)}, u32[]{:S(2)}) collective-permute-start(bf16[4,1,128,128]{3,2,0,1:T(8,128)(2,1)S(1)} %collective-permute-done.27), channel_id=1, source_target_pairs={{0,448},{64,0},{128,64},{192,128},{256,192},{320,256},{384,320},{4... | collective-permute-start | bytes 393224 | tf_op jit(solution)/shard_map/ppermute | solution.py:20
  337.1 9.6 %collective-permute-start.35 = (bf16[4,1,128,128]{3,2,0,1:T(8,128)(2,1)S(1)}, bf16[4,1,128,128]{3,2,0,1:T(8,128)(2,1)S(1)}, u32[]{:S(2)}, u32[]{:S(2)}) collective-permute-start(bf16[4,1,128,128]{3,2,0,1:T(8,128)(2,1)S(1)} %collective-permute-done.31), channel_id=1, source_target_pairs={{0,448},{64,0},{128,64},{192,128},{256,192},{320,256},{384,320},{4... | collective-permute-start | bytes 393224 | tf_op jit(solution)/shard_map/ppermute | solution.py:20
  347.4 16.8 %collective-permute-start.39 = (bf16[4,1,128,128]{3,2,0,1:T(8,128)(2,1)S(1)}, bf16[4,1,128,128]{3,2,0,1:T(8,128)(2,1)S(1)}, u32[]{:S(2)}, u32[]{:S(2)}) collective-permute-start(bf16[4,1,128,128]{3,2,0,1:T(8,128)(2,1)S(1)} %collective-permute-done.35), channel_id=1, source_target_pairs={{0,448},{64,0},{128,64},{192,128},{256,192},{320,256},{384,320},{4... | collective-permute-start | bytes 393224 | tf_op jit(solution)/shard_map/ppermute | solution.py:20
  364.9 17.4 %collective-permute-start.43 = (bf16[4,1,128,128]{3,2,0,1:T(8,128)(2,1)S(1)}, bf16[4,1,128,128]{3,2,0,1:T(8,128)(2,1)S(1)}, u32[]{:S(2)}, u32[]{:S(2)}) collective-permute-start(bf16[4,1,128,128]{3,2,0,1:T(8,128)(2,1)S(1)} %collective-permute-done.39), channel_id=1, source_target_pairs={{0,448},{64,0},{128,64},{192,128},{256,192},{320,256},{384,320},{4... | collective-permute-start | bytes 393224 | tf_op jit(solution)/shard_map/ppermute | solution.py:20
  375.3 10.0 %collective-permute-start.73 = (bf16[2,128,128]{2,1,0:T(8,128)(2,1)S(1)}, bf16[2,128,128]{2,1,0:T(8,128)(2,1)S(1)}, u32[]{:S(2)}, u32[]{:S(2)}) collective-permute-start(bf16[2,128,128]{2,1,0:T(8,128)(2,1)S(1)} %collective-permute-done.69), channel_id=1, source_target_pairs={{0,62},{2,0},{4,2},{6,4},{8,6},{10,8},{12,10},{14,12},{16,14},{18,... | collective-permute-start | bytes 196616 | tf_op jit(solution)/shard_map/ppermute | solution.py:20
  (88 other events, 730.7 us)
Sparse Core Ops, SparseCore 0:
  441.3 67.8 reduce-scatter.1
where the time goes:
time: 519 us; the launch traced here: 516 us
  starting transfers between devices  326 us (63%)
  waiting for transfers between devices  115 us (22%)
  local copies, waits for them, and re-layouts  28.5 us (5%)
  other arithmetic  17.8 us (3%)
  between operations  16.3 us (3%)
  matrix products  12.4 us (2%)
    ppermute x76, starting transfers between devices, passed_along(): lax.ppermute(value, axis, [(i, (i + by) % count) for i in range(count)])  326 us
    reduce_scatter x1, waiting for transfers between devices, per_device(): return lax.psum_scatter(total, 'layer', scatter_dimension=0, tiled=True)  68 us
    ppermute x76, waiting for transfers between devices, passed_along(): lax.ppermute(value, axis, [(i, (i + by) % count) for i in range(count)])  47.3 us
    another operation x32, other arithmetic  15.9 us
    reshape x16, local copies, waits for them, and re-layouts, dense_kernel(): tiles = flat.astype(jnp.bfloat16).reshape(BR, inner, block, block)  11.8 us
  transfers between devices with their start and end apart: 77, of which 30 were waited for; matrix products, arithmetic and copies ran while one was open for 10% of the time, Pallas kernels for 0%

commit v1 on v0

v1 whole, which is shorter than its diff:
```python
import jax
import jax.numpy as jnp
from jax import lax
from jax.experimental import pallas as pl
from jax.experimental.pallas import tpu as pltpu
from jax.sharding import PartitionSpec as P

MESH = pl.DeviceIdType.MESH
NY, NZ, NX, NL = 8, 8, 4, 2
B = 128

S_PATH = {
    (1, 0): (0, 0), (7, 0): (0, 0), (2, 0): (0, 0), (6, 0): (0, 0),
    (3, 0): (0, 0), (5, 0): (0, 0), (4, 0): (0, 0),
}
for _z in (0, 1, 7, 2, 6, 3, 5, 4):
    S_PATH[_z, 1] = (_z, 0)
    S_PATH[_z, 3] = (_z, 0)
for _z in (0, 1, 7, 2, 6, 3, 5, 4):
    S_PATH[_z, 2] = (_z, 1 if _z % 2 else 3)
S_ORDER = list(S_PATH)
X_PATH = {1: 0, 7: 0, 2: 0, 6: 0, 3: 2, 5: 6, 4: 2}
X_ORDER = [1, 7, 2, 6, 3, 5, 4]
EVENTS = None


def steps():
    s_steps = {(b[0] - a[0], b[1] - a[1]) for b, a in S_PATH.items()}
    x_steps = {b - a for b, a in X_PATH.items()}
    found = {(0, dz % NZ, dx % NX) for dz, dx in s_steps}
    found |= {(0, -dz % NZ, -dx % NX) for dz, dx in s_steps}
    found |= {(dy % NY, 0, 0) for dy in x_steps} | {(-dy % NY, 0, 0) for dy in x_steps}
    return sorted(found)


def kernel(s_hbm, ss_hbm, x_hbm, xs_hbm, out, sbuf, xbuf, sl, xl, dummy, ssm, xsm,
           s_sem, x_sem, sib_s, sib_x, send, local):
    y = lax.axis_index("row")
    col = lax.axis_index("col")
    l = lax.axis_index("layer")
    z, x = col // NX, col % NX
    sg = 1 - 2 * l

    def place(dy, dz, dx):
        return (
            lax.rem(y + sg * dy + NY, NY),
            lax.rem(z + sg * dz + NZ, NZ) * NX + lax.rem(x + sg * dx + NX, NX),
            l,
        )

    sibling = (y, col, 1 - l)
    peers = steps()
    barrier = pltpu.get_barrier_semaphore()
    for peer in peers:
        pl.semaphore_signal(barrier, inc=1, device_id=place(*peer), device_id_type=MESH)
    pl.semaphore_signal(barrier, inc=1, device_id=sibling, device_id_type=MESH)

    loads = [
        pltpu.make_async_copy(ss_hbm, ssm, local.at[0]),
        pltpu.make_async_copy(xs_hbm, xsm, local.at[1]),
        pltpu.make_async_copy(s_hbm.at[0, 0], sbuf.at[pl.ds(col * 2, 2)], local.at[2]),
        pltpu.make_async_copy(x_hbm.at[:, 0, 0, 0], xbuf.at[pl.ds(y * 4, 4)], local.at[3]),
    ]
    for load in loads:
        load.start()
    loads[0].wait()
    loads[1].wait()
    for a in range(2):
        sl[col * 2 + a] = jnp.full((1, B), ssm[0, 0, a], jnp.int32)
    for m in range(4):
        xl[y * 4 + m] = jnp.full((1, B), xsm[m, 0, 0, 0], jnp.int32)
    loads[2].wait()
    loads[3].wait()
    pl.semaphore_wait(barrier, len(peers) + 1)

    s_index = {o: i for i, o in enumerate(S_ORDER)}
    x_index = {o: i for i, o in enumerate(X_ORDER)}

    def s_origin(o):
        return lax.rem(z - sg * o[0] + NZ, NZ) * NX + lax.rem(x - sg * o[1] + NX, NX)

    def x_origin(o):
        return lax.rem(y - sg * o + NY, NY)

    def wait_bytes(ref, sem):
        pltpu.make_async_copy(ref, ref, sem).wait()

    def send_s(o):
        piece = s_origin(o)
        block = sbuf.at[pl.ds(piece * 2 + l, 1)]
        slots = sl.at[pl.ds(piece * 2, 2)]
        for child, parent in S_PATH.items():
            if parent == o:
                to = place(0, (child[0] - o[0]) % NZ, (child[1] - o[1]) % NX)
                got = s_sem.at[s_index[child]]
                pltpu.make_async_remote_copy(block, block, send.at[0], got, device_id=to, device_id_type=MESH).start()
                pltpu.make_async_remote_copy(slots, slots, send.at[1], got, device_id=to, device_id_type=MESH).start()
        if o != (0, 0):
            pltpu.make_async_remote_copy(
                block, block, send.at[2], sib_s.at[o[0] % NZ], device_id=sibling, device_id_type=MESH
            ).start()

    def send_x(o):
        origin = x_origin(o)
        block = xbuf.at[pl.ds(origin * 4 + l * 2, 2)]
        slots = xl.at[pl.ds(origin * 4, 4)]
        for child, parent in X_PATH.items():
            if parent == o:
                to = place((child - o) % NY, 0, 0)
                got = x_sem.at[x_index[child]]
                pltpu.make_async_remote_copy(block, block, send.at[3], got, device_id=to, device_id_type=MESH).start()
                pltpu.make_async_remote_copy(slots, slots, send.at[4], got, device_id=to, device_id_type=MESH).start()
        if o != 0:
            pltpu.make_async_remote_copy(
                block, block, send.at[5], sib_x, device_id=sibling, device_id_type=MESH
            ).start()

    send_s((0, 0))
    send_x(0)
    events = EVENTS
    if events is None:
        events = [("x", o) for o in X_ORDER[:4]] + [("s", o) for o in S_ORDER[:12]]
        events += [("x", o) for o in X_ORDER[4:]] + [("s", o) for o in S_ORDER[12:]]
    for kind, o in events:
        if kind == "s":
            wait_bytes(dummy.at[pl.ds(0, 66)], s_sem.at[s_index[o]])
            send_s(o)
        else:
            wait_bytes(dummy, x_sem.at[x_index[o]])
            send_x(o)
    wait_bytes(xbuf.at[pl.ds(0, 14)], sib_x)

    def group(g, first):
        zz = lax.rem(z + sg * g + NZ, NZ)
        m, base = zz // 2, lax.rem(zz, 2) * 4
        x_tiles, masks, blocks = [], [], []
        for c in range(NX):
            xv = xbuf[(base + c) * 4 + m]
            xs = xl[(base + c) * 4 + m]
            odd = xs & 1
            put = jnp.broadcast_to(odd.astype(jnp.float32), (16, B)).astype(jnp.bfloat16)[None]
            keep = jnp.broadcast_to((1 - odd).astype(jnp.float32), (16, B)).astype(jnp.bfloat16)[None]
            parts = xv.reshape(8, 16, B)
            x_tiles.append(jnp.concatenate([(parts * keep).reshape(B, B), (parts * put).reshape(B, B)], axis=1))
            first_row = l * 8 + (xs >> 1)
            masks.append([sl[(zz * NX + c) * 2 + a] - first_row for a in range(2)])
            blocks.append([sbuf[(zz * NX + c) * 2 + a].reshape(8, 16, B) for a in range(2)])
        x_tile = jnp.concatenate(x_tiles, axis=0)
        for br in range(4):
            row = []
            for c in range(NX):
                hit = [
                    jnp.broadcast_to((masks[c][a] == 2 * br).astype(jnp.float32), (16, B)).astype(jnp.bfloat16)[None]
                    for a in range(2)
                ]
                row.append((blocks[c][0] * hit[0] + blocks[c][1] * hit[1]).reshape(B, B))
            part = jnp.dot(jnp.concatenate(row, axis=1), x_tile, preferred_element_type=jnp.float32)
            if first:
                out[pl.ds(br * B, B), :] = part
            else:
                out[pl.ds(br * B, B), :] += part

    for i, g in enumerate((0, 1, 7, 2, 6, 3, 5, 4)):
        wait_bytes(sbuf.at[pl.ds(0, 3 if g == 0 else 4)], sib_s.at[g])
        group(g, i == 0)
    wait_bytes(sbuf.at[pl.ds(0, 31)], send.at[0])
    wait_bytes(sl.at[pl.ds(0, 62)], send.at[1])
    wait_bytes(sbuf.at[pl.ds(0, 31)], send.at[2])
    wait_bytes(xbuf.at[pl.ds(0, 14)], send.at[3])
    wait_bytes(xl.at[pl.ds(0, 28)], send.at[4])
    wait_bytes(xbuf.at[pl.ds(0, 14)], send.at[5])


def per_device(s_values, s_slots, x_values, x_slots):
    return pl.pallas_call(
        kernel,
        out_shape=jax.ShapeDtypeStruct((512, 256), jnp.float32),
        in_specs=[pl.BlockSpec(memory_space=pl.ANY)] * 4,
        out_specs=pl.BlockSpec(memory_space=pltpu.VMEM),
        scratch_shapes=[
            pltpu.VMEM((64, B, B), jnp.bfloat16),
            pltpu.VMEM((32, B, B), jnp.bfloat16),
            pltpu.VMEM((64, 1, B), jnp.int32),
            pltpu.VMEM((32, 1, B), jnp.int32),
            pltpu.VMEM((132, 1, B), jnp.int32),
            pltpu.SMEM((1, 1, 2), jnp.int32),
            pltpu.SMEM((4, 1, 1, 1), jnp.int32),
            pltpu.SemaphoreType.DMA((31,)),
            pltpu.SemaphoreType.DMA((7,)),
            pltpu.SemaphoreType.DMA((8,)),
            pltpu.SemaphoreType.DMA,
            pltpu.SemaphoreType.DMA((6,)),
            pltpu.SemaphoreType.DMA((4,)),
        ],
        compiler_params=pltpu.CompilerParams(
            collective_id=0, has_side_effects=True, vmem_limit_bytes=48 * 2**20
        ),
        cost_estimate=pl.CostEstimate(flops=2**30, bytes_accessed=2**20, transcendentals=0),
        name="block_product",
    )(s_values, s_slots, x_values, x_slots)


def solution(mesh):
    placed = (
        P("row", "col", None, None, None),
        P("row", "col", None),
        P(None, "row", "col", None, None, None),
        P(None, "row", "col", None),
    )
    return jax.shard_map(
        per_device,
        mesh=mesh,
        in_specs=placed,
        out_specs=P(("row", "layer"), "col"),
        check_vma=False,
    )
```

time: 519 us -> 36.2 us (0.07)
  starting transfers between devices: 326 us -> 0 us
  waiting for transfers between devices: 115 us -> 0 us
  Pallas kernels: 0 us -> 32.7 us
  local copies, waits for them, and re-layouts: 28.5 us -> 3.3 us
  other arithmetic: 17.8 us -> 0 us
  between operations: 16.3 us -> 0.01 us
  matrix products: 12.4 us -> 0 us
    ppermute x76 -> x0, starting transfers between devices: 326 us -> none  [passed_along(): lax.ppermute(value, axis, [(i, (i + by) % count) for i in range(count)])]
    reduce_scatter x1 -> x0, waiting for transfers between devices: 68 us -> none  [per_device(): return lax.psum_scatter(total, 'layer', scatter_dimension=0, tiled=True)]
    ppermute x76 -> x0, waiting for transfers between devices: 47.3 us -> none  [passed_along(): lax.ppermute(value, axis, [(i, (i + by) % count) for i in range(count)])]
    pallas_call x0 -> x1, Pallas kernels: none -> 32.7 us  [per_device(): pl.pallas_call(kernel, out_shape=jax.ShapeDtypeStruct((512, 256), jnp.flo...]
    another operation x32 -> x0, other arithmetic: 15.9 us -> none
    dot_general x32 -> x0, matrix products: 12.4 us -> none  [the longest x16 6.63 us: dense_kernel(): return total + jnp.dot(s_tile, x_tile, preferred_element_type=jnp.float32)]
    reshape x16 -> x0, local copies, waits for them, and re-layouts: 11.8 us -> none  [dense_kernel(): tiles = flat.astype(jnp.bfloat16).reshape(BR, inner, block, block)]
    dynamic_slice x16 -> x0, local copies, waits for them, and re-layouts: 9.36 us -> none  [per_device(): lax.dynamic_index_in_dim(held_x[1], group_pick, 0, keepdims=False)]
  transfers between devices with their start and end apart: 77 -> 0, of which waited for: 30 -> 0; matrix products, arithmetic and copies ran while one was open for 10% -> 0% of each run, Pallas kernels for 0% -> 0%
where the time goes in v1:
time: 36.2 us; the launch traced here: 36 us
  Pallas kernels  32.7 us (90%)
  local copies, waits for them, and re-layouts  3.3 us (9%)
    pallas_call x1, Pallas kernels, per_device(): pl.pallas_call(kernel, out_shape=jax.ShapeDtypeStruct((512, 256), jnp.flo...  32.7 us
    unnamed x8, local copies, waits for them, and re-layouts  3.3 us

profile of v1, /device:TPU:1, one launch (start us, length us, event | category | flops | bytes accessed | tf_op | source)
XLA Modules:
  0.0 36.0 jit_solution(17343167835609779876)
XLA Ops:
  0.0 0.0 copy-start.2
  0.0 0.8 %copy.5.xs_hbm = s32[4,1,1,1]{3,2,1,0:T(1,128)S(1)} copy(s32[4,1,1,1]{0,3,2,1:T(1,128)} %param.7) | data formatting | bytes 32 | tf_op args[3]
  0.8 0.0 copy-done.2
  0.8 0.0 copy-start
  0.8 0.9 %copy-done = bf16[4,1,1,1,128,128]{5,4,3,2,1,0:T(8,128)(2,1)S(1)} copy-done((bf16[4,1,1,1,128,128]{5,4,3,2,1,0:T(8,128)(2,1)S(1)}, bf16[4,1,1,1,128,128]{5,4,3,2,1,0:T(8,128)(2,1)}, u32[]{:S(2)}) %copy-start) | copy-done | bytes 131096
  1.7 0.0 copy-start.1
  1.7 0.8 %copy-done.1 = bf16[1,1,2,128,128]{4,3,2,1,0:T(8,128)(2,1)S(1)} copy-done((bf16[1,1,2,128,128]{4,3,2,1,0:T(8,128)(2,1)S(1)}, bf16[1,1,2,128,128]{4,3,2,1,0:T(8,128)(2,1)}, u32[]{:S(2)}) %copy-start.1) | copy-done | bytes 65560
  2.5 32.7 %block_product.1 = f32[512,256]{1,0:T(8,128)S(1)} custom-call(bf16[1,1,2,128,128]{4,3,2,1,0:T(8,128)(2,1)S(1)} %copy-done.1, s32[1,1,2]{2,1,0:T(1,128)S(1)} %copy-done.2, bf16[4,1,1,1,128,128]{5,4,3,2,1,0:T(8,128)(2,1)S(1)} %copy-done, s32[4,1,1,1]{3,2,1,0:T(1,128)S(1)} %copy.5.xs_hbm), custom_call_target="tpu_custom_call" | custom-call | flops 1073741824 | bytes 1048576 | tf_op jit(solution)/shard_map/block_product/pallas_call | solution.py:175
  35.2 0.8 %copy.7 = f32[512,256]{1,0:T(8,128)} copy(f32[512,256]{1,0:T(8,128)S(1)} %block_product.1) | data formatting | bytes 1048576
Async XLA Ops:
  0.0 0.8 %copy-start.2 = (s32[1,1,2]{2,1,0:T(1,128)S(1)}, s32[1,1,2]{2,1,0:T(1,128)}, u32[]{:S(2)}) copy-start(s32[1,1,2]{2,1,0:T(1,128)} %ss_hbm.1) | copy-start | bytes 28
  0.8 0.9 %copy-start = (bf16[4,1,1,1,128,128]{5,4,3,2,1,0:T(8,128)(2,1)S(1)}, bf16[4,1,1,1,128,128]{5,4,3,2,1,0:T(8,128)(2,1)}, u32[]{:S(2)}) copy-start(bf16[4,1,1,1,128,128]{5,4,3,2,1,0:T(8,128)(2,1)} %x_hbm.1) | copy-start | bytes 393220
  1.7 0.8 %copy-start.1 = (bf16[1,1,2,128,128]{4,3,2,1,0:T(8,128)(2,1)S(1)}, bf16[1,1,2,128,128]{4,3,2,1,0:T(8,128)(2,1)}, u32[]{:S(2)}) copy-start(bf16[1,1,2,128,128]{4,3,2,1,0:T(8,128)(2,1)} %s_hbm.1) | copy-start | bytes 196612

commit v2 on v1

v2 whole, which is shorter than its diff:
```python
import jax
import jax.numpy as jnp
from jax import lax
from jax.experimental import pallas as pl
from jax.experimental.pallas import tpu as pltpu
from jax.sharding import PartitionSpec as P

MESH = pl.DeviceIdType.MESH
NY, NZ, NX = 8, 8, 4
B = 128
Y_PATH = {1: 0, 7: 0, 2: 0, 6: 0, 3: 2, 5: 6, 4: 2}
Y_ORDER = [1, 7, 2, 6, 3, 5, 4]
Y_STEPS = (1, 7, 2, 6)


def kernel(s_hbm, ss_hbm, x_hbm, xs_hbm, out, sbuf, xbuf, sl, xl, dummy, ssm, xsm,
           z_sem, x_sem, y_sem, sib_s, sib_x, send, local, ready):
    y = lax.axis_index("row")
    col = lax.axis_index("col")
    l = lax.axis_index("layer")
    z, x = col // NX, col % NX
    sg = 1 - 2 * l

    def on_z(to):
        return (y, to * NX + x, l)

    def on_x(step):
        return (y, z * NX + lax.rem(x + step, NX), l)

    def on_y(step):
        return (lax.rem(y + sg * step + NY, NY), col, l)

    sibling = (y, col, 1 - l)

    barrier = pltpu.get_barrier_semaphore()
    greeted = [sibling] + [on_x(s) for s in (1, 2, 3)] + [on_y(s) for s in Y_STEPS]
    for peer in greeted:
        pl.semaphore_signal(barrier, inc=1, device_id=peer, device_id_type=MESH)
    for to in range(1, NZ):
        @pl.when(z < to)
        def _():
            pl.semaphore_signal(barrier, inc=1, device_id=on_z(to), device_id_type=MESH)

    own = (l * NZ + z) * NX + x
    loads = [
        pltpu.make_async_copy(ss_hbm, ssm, local.at[0]),
        pltpu.make_async_copy(xs_hbm, xsm, local.at[1]),
        pltpu.make_async_copy(s_hbm.at[0, 0, pl.ds(l, 1)], sbuf.at[pl.ds(own, 1)], local.at[2]),
        pltpu.make_async_copy(
            x_hbm.at[pl.ds(l * 2, 2), 0, 0, 0], xbuf.at[pl.ds((l * NY + y) * 2, 2)], local.at[3]
        ),
    ]
    for load in loads:
        load.start()
    loads[0].wait()
    loads[1].wait()
    for a in range(2):
        sl[col * 2 + a] = jnp.full((1, B), ssm[0, 0, a], jnp.int32)
    for m in range(4):
        xl[y * 4 + m] = jnp.full((1, B), xsm[0, 0, 0, m], jnp.int32)
    pl.semaphore_wait(barrier, len(greeted) + z)
    for to in range(NZ - 1):
        @pl.when(z > to)
        def _():
            pl.semaphore_signal(ready.at[z], inc=1, device_id=on_z(to), device_id_type=MESH)

    def remote(source, target, sent, got, to):
        pltpu.make_async_remote_copy(source, target, sent, got, device_id=to, device_id_type=MESH).start()

    def wait_bytes(ref, sem):
        pltpu.make_async_copy(ref, ref, sem).wait()

    def rows(n):
        return dummy.at[pl.ds(0, n)]

    def send_z(to):
        slots = sl.at[pl.ds(col * 2, 2)]
        remote(s_hbm.at[0, 0, pl.ds(l, 1)], sbuf.at[pl.ds(own, 1)], send.at[0], z_sem.at[z], on_z(to))
        remote(slots, slots, send.at[1], z_sem.at[z], on_z(to))

    def send_x(zs, first):
        block = sbuf.at[pl.ds((l * NZ + zs) * NX + x, 1)]
        slots = sl.at[pl.ds((zs * NX + x) * 2, 2)]
        for step in (2, 1, 3):
            source = s_hbm.at[0, 0, pl.ds(l, 1)] if first else block
            remote(source, block, send.at[0], x_sem.at[zs], on_x(step))
            remote(slots, slots, send.at[1], x_sem.at[zs], on_x(step))

    def send_y(o):
        origin = lax.rem(y - sg * o + NY, NY)
        block = xbuf.at[pl.ds((l * NY + origin) * 2, 2)]
        slots = xl.at[pl.ds(origin * 4, 4)]
        for child, parent in Y_PATH.items():
            if parent == o:
                to = on_y((child - o) % NY)
                got = y_sem.at[Y_ORDER.index(child)]
                source = x_hbm.at[pl.ds(l * 2, 2), 0, 0, 0] if o == 0 else block
                remote(source, block, send.at[3], got, to)
                remote(slots, slots, send.at[4], got, to)

    def share_y(o):
        origin = lax.rem(y - sg * o + NY, NY)
        block = xbuf.at[pl.ds((l * NY + origin) * 2, 2)]
        remote(block, block, send.at[5], sib_x, sibling)

    def group(zs):
        x_tiles, targets, blocks = [], [], []
        for c in range(NX):
            r = (zs % 2) * 4 + c
            m = zs // 2
            xv = xbuf[((m // 2) * NY + r) * 2 + m % 2].reshape(8, 16, B)
            xs = xl[r * 4 + m]
            odd = xs & 1
            put = jnp.broadcast_to(odd.astype(jnp.float32), (16, B)).astype(jnp.bfloat16)[None]
            keep = jnp.broadcast_to((1 - odd).astype(jnp.float32), (16, B)).astype(jnp.bfloat16)[None]
            x_tiles.append(jnp.concatenate([(xv * keep).reshape(B, B), (xv * put).reshape(B, B)], axis=1))
            first_row = l * 8 + (xs >> 1)
            targets.append([sl[(zs * NX + c) * 2 + a] - first_row for a in range(2)])
            blocks.append([sbuf[(a * NZ + zs) * NX + c].reshape(8, 16, B) for a in range(2)])
        x_tile = jnp.concatenate(x_tiles, axis=0)
        for br in range(4):
            row = []
            for c in range(NX):
                hit = [
                    jnp.broadcast_to((targets[c][a] == 2 * br).astype(jnp.float32), (16, B)).astype(jnp.bfloat16)[None]
                    for a in range(2)
                ]
                row.append((blocks[c][0] * hit[0] + blocks[c][1] * hit[1]).reshape(B, B))
            part = jnp.dot(jnp.concatenate(row, axis=1), x_tile, preferred_element_type=jnp.float32)
            if zs == 0:
                out[pl.ds(br * B, B), :] = part
            else:
                out[pl.ds(br * B, B), :] += part

    def product(zs):
        wait_bytes(sbuf.at[pl.ds(0, NX)], sib_s.at[zs])
        group(zs)

    def share_s(zs):
        wait_bytes(rows(198), x_sem.at[zs])
        blocks = sbuf.at[pl.ds((l * NZ + zs) * NX, NX)]
        remote(blocks, blocks, send.at[2], sib_s.at[zs], sibling)

    def send_when_ready(to):
        pl.semaphore_wait(ready.at[to], 1)
        send_z(to)

    def pass_x(zs):
        @pl.when(z != zs)
        def _():
            wait_bytes(rows(66), z_sem.at[zs])
            send_x(zs, False)

    def pass_y(o):
        wait_bytes(rows(132), y_sem.at[Y_ORDER.index(o)])
        send_y(o)
        share_y(o)

    for to in range(NZ - 1):
        @pl.when(z > to)
        def _():
            send_z(to)
    send_x(z, True)
    send_y(0)
    loads[2].wait()
    loads[3].wait()
    share_y(0)
    half = NZ // 2

    @pl.when(z < half)
    def _():
        for zs in range(half):
            @pl.when(z < zs)
            def _():
                send_when_ready(zs)

            pass_x(zs)
        for o in Y_ORDER[:4]:
            pass_y(o)
        for zs in range(half, NZ):
            send_when_ready(zs)
        for zs in range(half, NZ):
            pass_x(zs)

    @pl.when(z >= half)
    def _():
        for zs in range(half + 1, NZ):
            @pl.when(z < zs)
            def _():
                send_when_ready(zs)
        for zs in range(half, NZ):
            pass_x(zs)
        for zs in range(half):
            pass_x(zs)
        for o in Y_ORDER[:4]:
            pass_y(o)

    for o in Y_ORDER[4:]:
        pass_y(o)
    for zs in range(half):
        share_s(zs)
    wait_bytes(xbuf.at[pl.ds(0, 16)], sib_x)
    for zs in range(half):
        product(zs)
    for zs in range(half, NZ):
        share_s(zs)
    for zs in range(half, NZ):
        product(zs)
    wait_bytes(sbuf.at[pl.ds(0, 31)], send.at[0])
    wait_bytes(sl.at[pl.ds(0, 62)], send.at[1])
    wait_bytes(sbuf.at[pl.ds(0, 32)], send.at[2])
    wait_bytes(xbuf.at[pl.ds(0, 14)], send.at[3])
    wait_bytes(xl.at[pl.ds(0, 28)], send.at[4])
    wait_bytes(xbuf.at[pl.ds(0, 16)], send.at[5])


def per_device(s_values, s_slots, x_values, x_slots):
    return pl.pallas_call(
        kernel,
        out_shape=jax.ShapeDtypeStruct((512, 256), jnp.float32),
        in_specs=[pl.BlockSpec(memory_space=pl.ANY)] * 4,
        out_specs=pl.BlockSpec(memory_space=pltpu.VMEM),
        scratch_shapes=[
            pltpu.VMEM((64, B, B), jnp.bfloat16),
            pltpu.VMEM((32, B, B), jnp.bfloat16),
            pltpu.VMEM((64, 1, B), jnp.int32),
            pltpu.VMEM((32, 1, B), jnp.int32),
            pltpu.VMEM((198, 1, B), jnp.int32),
            pltpu.SMEM((1, 1, 2), jnp.int32),
            pltpu.SMEM((1, 1, 1, 4), jnp.int32),
            pltpu.SemaphoreType.DMA((8,)),
            pltpu.SemaphoreType.DMA((8,)),
            pltpu.SemaphoreType.DMA((7,)),
            pltpu.SemaphoreType.DMA((8,)),
            pltpu.SemaphoreType.DMA,
            pltpu.SemaphoreType.DMA((6,)),
            pltpu.SemaphoreType.DMA((4,)),
            pltpu.SemaphoreType.REGULAR((8,)),
        ],
        compiler_params=pltpu.CompilerParams(
            collective_id=0, has_side_effects=True, vmem_limit_bytes=62 * 2**20
        ),
        cost_estimate=pl.CostEstimate(flops=2**30, bytes_accessed=2**20, transcendentals=0),
        name="block_product",
    )(s_values, s_slots, x_values, x_slots.transpose(1, 2, 3, 0))


def solution(mesh):
    placed = (
        P("row", "col", None, None, None),
        P("row", "col", None),
        P(None, "row", "col", None, None, None),
        P(None, "row", "col", None),
    )
    return jax.shard_map(
        per_device,
        mesh=mesh,
        in_specs=placed,
        out_specs=P(("row", "layer"), "col"),
        check_vma=False,
    )
```

time: 36.2 us -> 32 us (0.88)
  the two profiles are of different devices: /device:TPU:1 before, /device:TPU:257 now
where the time goes in v2:
time: 32 us; the launch traced here: 31.8 us
  Pallas kernels  29.9 us (93%)
  local copies, waits for them, and re-layouts  1.87 us (6%)
    pallas_call x1, Pallas kernels, per_device(): pl.pallas_call(kernel, out_shape=jax.ShapeDtypeStruct((512, 256), jnp.flo...  29.9 us
    unnamed x1, local copies, waits for them, and re-layouts  1.87 us

profile of v2, /device:TPU:257, one launch (start us, length us, event | category | flops | bytes accessed | tf_op | source)
XLA Modules:
  0.0 31.8 jit_solution(16907544098983853169)
XLA Ops:
  0.0 29.9 %block_product.1 = f32[512,256]{1,0:T(8,128)} custom-call(bf16[1,1,2,128,128]{4,3,2,1,0:T(8,128)(2,1)} %s_hbm.1, s32[1,1,2]{2,1,0:T(1,128)} %ss_hbm.1, bf16[4,1,1,1,128,128]{5,4,3,2,1,0:T(8,128)(2,1)} %x_hbm.1, s32[1,1,1,4]{3,2,1,0:T(1,128)} %bitcast.1), custom_call_target="tpu_custom_call" | custom-call | flops 1073741824 | bytes 1048576 | tf_op jit(solution)/shard_map/block_product/pallas_call | solution.py:218
  29.9 1.9 %copy.6 = f32[512,256]{1,0:T(8,128)} copy(f32[512,256]{1,0:T(8,128)} %block_product.1) | data formatting | bytes 1048576

commit v3 on v2

--- a/solution.py
+++ b/solution.py
@@ -181,6 +181,10 @@
             send_when_ready(zs)
         for zs in range(half, NZ):
             pass_x(zs)
+        for o in Y_ORDER[4:]:
+            pass_y(o)
+        for zs in range(half):
+            share_s(zs)
 
     @pl.when(z >= half)
     def _():
@@ -190,20 +194,26 @@
                 send_when_ready(zs)
         for zs in range(half, NZ):
             pass_x(zs)
-        for zs in range(half):
-            pass_x(zs)
         for o in Y_ORDER[:4]:
             pass_y(o)
-
-    for o in Y_ORDER[4:]:
-        pass_y(o)
-    for zs in range(half):
-        share_s(zs)
+        for zs in range(half):
+            pass_x(zs)
+        for o in Y_ORDER[4:]:
+            pass_y(o)
+        for zs in range(half, NZ):
+            share_s(zs)
+        for zs in range(half):
+            share_s(zs)
+
     wait_bytes(xbuf.at[pl.ds(0, 16)], sib_x)
     for zs in range(half):
         product(zs)
-    for zs in range(half, NZ):
-        share_s(zs)
+
+    @pl.when(z < half)
+    def _():
+        for zs in range(half, NZ):
+            share_s(zs)
+
     for zs in range(half, NZ):
         product(zs)
     wait_bytes(sbuf.at[pl.ds(0, 31)], send.at[0])

time: 32 us -> 31.3 us (0.978)
  Pallas kernels: 29.9 us -> 29.3 us
    pallas_call x1, Pallas kernels: 29.9 us -> 29.3 us  [per_device(): pl.pallas_call(kernel, out_shape=jax.ShapeDtypeStruct((512, 256), jnp.flo...]
where the time goes in v3:
time: 31.3 us; the launch traced here: 31.1 us
  Pallas kernels  29.3 us (94%)
  local copies, waits for them, and re-layouts  1.87 us (6%)
    pallas_call x1, Pallas kernels, per_device(): pl.pallas_call(kernel, out_shape=jax.ShapeDtypeStruct((512, 256), jnp.flo...  29.3 us
    unnamed x1, local copies, waits for them, and re-layouts  1.87 us

profile of v3, /device:TPU:257, one launch (start us, length us, event | category | flops | bytes accessed | tf_op | source)
XLA Modules:
  0.0 31.1 jit_solution(3393949592932235911)
XLA Ops:
  0.0 29.3 %block_product.1 = f32[512,256]{1,0:T(8,128)} custom-call(bf16[1,1,2,128,128]{4,3,2,1,0:T(8,128)(2,1)} %s_hbm.1, s32[1,1,2]{2,1,0:T(1,128)} %ss_hbm.1, bf16[4,1,1,1,128,128]{5,4,3,2,1,0:T(8,128)(2,1)} %x_hbm.1, s32[1,1,1,4]{3,2,1,0:T(1,128)} %bitcast.1), custom_call_target="tpu_custom_call" | custom-call | flops 1073741824 | bytes 1048576 | tf_op jit(solution)/shard_map/block_product/pallas_call | solution.py:228
  29.3 1.9 %copy.6 = f32[512,256]{1,0:T(8,128)} copy(f32[512,256]{1,0:T(8,128)} %block_product.1) | data formatting | bytes 1048576

commit v4 on v2

--- a/solution.py
+++ b/solution.py
@@ -11,10 +11,33 @@
 Y_PATH = {1: 0, 7: 0, 2: 0, 6: 0, 3: 2, 5: 6, 4: 2}
 Y_ORDER = [1, 7, 2, 6, 3, 5, 4]
 Y_STEPS = (1, 7, 2, 6)
+LOW = (
+    ("y", (1, 7, 2, 6,)),
+    ("r", (1,)),
+    ("z", (1,)),
+    ("r", (2,)),
+    ("z", (2,)),
+    ("r", (3,)),
+    ("z", (3, 0,)),
+    ("d", (1, 7, 2, 6,)),
+    ("r", (4, 5, 6, 7,)),
+    ("z", (4, 5, 6, 7,)),
+    ("d", (3, 5, 4,)),
+    ("s", (0, 1, 2, 3, 4, 5, 6, 7,)),
+)
+HIGH = (
+    ("y", (1, 7, 2, 6,)),
+    ("r", (5, 6, 7,)),
+    ("z", (4, 5, 6, 7,)),
+    ("d", (1, 7, 2, 6,)),
+    ("z", (0, 1, 2, 3,)),
+    ("d", (3, 5, 4,)),
+    ("s", (4, 5, 6, 7, 0, 1, 2, 3,)),
+)
 
 
 def kernel(s_hbm, ss_hbm, x_hbm, xs_hbm, out, sbuf, xbuf, sl, xl, dummy, ssm, xsm,
-           z_sem, x_sem, y_sem, sib_s, sib_x, send, local, ready):
+           z_sem, x_sem, y_sem, sib_s, sib_x, send, local, ready, y_ready):
     y = lax.axis_index("row")
     col = lax.axis_index("col")
     l = lax.axis_index("layer")
@@ -32,14 +55,26 @@
 
     sibling = (y, col, 1 - l)
 
+    def rank(at):
+        return jnp.where(at < NY // 2, at, NY + 3 - at)
+
+    y_rank = rank(y)
+    other = {s: rank(on_y(s)[0]) for s in Y_STEPS}
     barrier = pltpu.get_barrier_semaphore()
-    greeted = [sibling] + [on_x(s) for s in (1, 2, 3)] + [on_y(s) for s in Y_STEPS]
+    greeted = [sibling] + [on_x(s) for s in (1, 2, 3)]
     for peer in greeted:
         pl.semaphore_signal(barrier, inc=1, device_id=peer, device_id_type=MESH)
     for to in range(1, NZ):
         @pl.when(z < to)
         def _():
             pl.semaphore_signal(barrier, inc=1, device_id=on_z(to), device_id_type=MESH)
+    for s in Y_STEPS:
+        @pl.when(y_rank < other[s])
+        def _():
+            pl.semaphore_signal(barrier, inc=1, device_id=on_y(s), device_id_type=MESH)
+    expected = len(greeted) + z
+    for s in Y_STEPS:
+        expected = expected + jnp.where(y_rank > other[s], 1, 0)
 
     own = (l * NZ + z) * NX + x
     loads = [
@@ -58,11 +93,18 @@
         sl[col * 2 + a] = jnp.full((1, B), ssm[0, 0, a], jnp.int32)
     for m in range(4):
         xl[y * 4 + m] = jnp.full((1, B), xsm[0, 0, 0, m], jnp.int32)
-    pl.semaphore_wait(barrier, len(greeted) + z)
+    pl.semaphore_wait(barrier, expected)
     for to in range(NZ - 1):
         @pl.when(z > to)
         def _():
             pl.semaphore_signal(ready.at[z], inc=1, device_id=on_z(to), device_id_type=MESH)
+
+    for s in Y_STEPS:
+        @pl.when(y_rank > other[s])
+        def _():
+            pl.semaphore_signal(
+                y_ready.at[Y_STEPS.index(-s % NY)], inc=1, device_id=on_y(s), device_id_type=MESH
+            )
 
     def remote(source, target, sent, got, to):
         pltpu.make_async_remote_copy(source, target, sent, got, device_id=to, device_id_type=MESH).start()
@@ -86,12 +128,12 @@
             remote(source, block, send.at[0], x_sem.at[zs], on_x(step))
             remote(slots, slots, send.at[1], x_sem.at[zs], on_x(step))
 
-    def send_y(o):
+    def send_y(o, only=None):
         origin = lax.rem(y - sg * o + NY, NY)
         block = xbuf.at[pl.ds((l * NY + origin) * 2, 2)]
         slots = xl.at[pl.ds(origin * 4, 4)]
         for child, parent in Y_PATH.items():
-            if parent == o:
+            if parent == o and only in (None, child):
                 to = on_y((child - o) % NY)
                 got = y_sem.at[Y_ORDER.index(child)]
                 source = x_hbm.at[pl.ds(l * 2, 2), 0, 0, 0] if o == 0 else block
@@ -156,55 +198,46 @@
         send_y(o)
         share_y(o)
 
+    def own_y(step):
+        @pl.when(y_rank < other[step])
+        def _():
+            pl.semaphore_wait(y_ready.at[Y_STEPS.index(step)], 1)
+        send_y(0, step)
+
+    def run(order):
+        for kind, k in [(kind, k) for kind, ks in order for k in ks]:
+            if kind == "y":
+                own_y(k)
+            elif kind == "r":
+                @pl.when(z < k)
+                def _():
+                    send_when_ready(k)
+            elif kind == "z":
+                pass_x(k)
+            elif kind == "d":
+                pass_y(k)
+            else:
+                share_s(k)
+
     for to in range(NZ - 1):
         @pl.when(z > to)
         def _():
             send_z(to)
     send_x(z, True)
-    send_y(0)
     loads[2].wait()
     loads[3].wait()
     share_y(0)
-    half = NZ // 2
-
-    @pl.when(z < half)
+
+    @pl.when(z < NZ // 2)
     def _():
-        for zs in range(half):
-            @pl.when(z < zs)
-            def _():
-                send_when_ready(zs)
-
-            pass_x(zs)
-        for o in Y_ORDER[:4]:
-            pass_y(o)
-        for zs in range(half, NZ):
-            send_when_ready(zs)
-        for zs in range(half, NZ):
-            pass_x(zs)
-
-    @pl.when(z >= half)
+        run(LOW)
+
+    @pl.when(z >= NZ // 2)
     def _():
-        for zs in range(half + 1, NZ):
-            @pl.when(z < zs)
-            def _():
-                send_when_ready(zs)
-        for zs in range(half, NZ):
-            pass_x(zs)
-        for zs in range(half):
-            pass_x(zs)
-        for o in Y_ORDER[:4]:
-            pass_y(o)
-
-    for o in Y_ORDER[4:]:
-        pass_y(o)
-    for zs in range(half):
-        share_s(zs)
+        run(HIGH)
+
     wait_bytes(xbuf.at[pl.ds(0, 16)], sib_x)
-    for zs in range(half):
-        product(zs)
-    for zs in range(half, NZ):
-        share_s(zs)
-    for zs in range(half, NZ):
+    for zs in range(NZ):
         product(zs)
     wait_bytes(sbuf.at[pl.ds(0, 31)], send.at[0])
     wait_bytes(sl.at[pl.ds(0, 62)], send.at[1])
@@ -236,6 +269,7 @@
             pltpu.SemaphoreType.DMA((6,)),
             pltpu.SemaphoreType.DMA((4,)),
             pltpu.SemaphoreType.REGULAR((8,)),
+            pltpu.SemaphoreType.REGULAR((4,)),
         ],
         compiler_params=pltpu.CompilerParams(
             collective_id=0, has_side_effects=True, vmem_limit_bytes=62 * 2**20

time: 32 us -> 28.5 us (0.89)
  Pallas kernels: 29.9 us -> 26.4 us
    pallas_call x1, Pallas kernels: 29.9 us -> 26.4 us  [per_device(): pl.pallas_call(kernel, out_shape=jax.ShapeDtypeStruct((512, 256), jnp.flo...]
where the time goes in v4:
time: 28.5 us; the launch traced here: 28.3 us
  Pallas kernels  26.4 us (93%)
  local copies, waits for them, and re-layouts  1.87 us (7%)
    pallas_call x1, Pallas kernels, per_device(): pl.pallas_call(kernel, out_shape=jax.ShapeDtypeStruct((512, 256), jnp.flo...  26.4 us
    unnamed x1, local copies, waits for them, and re-layouts  1.87 us

profile of v4, /device:TPU:257, one launch (start us, length us, event | category | flops | bytes accessed | tf_op | source)
XLA Modules:
  0.0 28.3 jit_solution(18071871394226968805)
XLA Ops:
  0.0 26.4 %block_product.1 = f32[512,256]{1,0:T(8,128)} custom-call(bf16[1,1,2,128,128]{4,3,2,1,0:T(8,128)(2,1)} %s_hbm.1, s32[1,1,2]{2,1,0:T(1,128)} %ss_hbm.1, bf16[4,1,1,1,128,128]{5,4,3,2,1,0:T(8,128)(2,1)} %x_hbm.1, s32[1,1,1,4]{3,2,1,0:T(1,128)} %bitcast.1), custom_call_target="tpu_custom_call" | custom-call | flops 1073741824 | bytes 1048576 | tf_op jit(solution)/shard_map/block_product/pallas_call | solution.py:251
  26.4 1.9 %copy.6 = f32[512,256]{1,0:T(8,128)} copy(f32[512,256]{1,0:T(8,128)} %block_product.1) | data formatting | bytes 1048576

commit v5 on v4

--- a/solution.py
+++ b/solution.py
@@ -247,8 +247,23 @@
     wait_bytes(xbuf.at[pl.ds(0, 16)], send.at[5])
 
 
+PARTS = 4
+
+
+def hand_over(made, out, sem):
+    rows = out.shape[0] // PARTS
+    copies = [
+        pltpu.make_async_copy(made.at[pl.ds(i * rows, rows)], out.at[pl.ds(i * rows, rows)], sem.at[i])
+        for i in range(PARTS)
+    ]
+    for copy in copies:
+        copy.start()
+    for copy in copies:
+        copy.wait()
+
+
 def per_device(s_values, s_slots, x_values, x_slots):
-    return pl.pallas_call(
+    made = pl.pallas_call(
         kernel,
         out_shape=jax.ShapeDtypeStruct((512, 256), jnp.float32),
         in_specs=[pl.BlockSpec(memory_space=pl.ANY)] * 4,
@@ -277,6 +292,15 @@
         cost_estimate=pl.CostEstimate(flops=2**30, bytes_accessed=2**20, transcendentals=0),
         name="block_product",
     )(s_values, s_slots, x_values, x_slots.transpose(1, 2, 3, 0))
+    return pl.pallas_call(
+        hand_over,
+        out_shape=jax.ShapeDtypeStruct((512, 256), jnp.float32),
+        in_specs=[pl.BlockSpec(memory_space=pl.ANY)],
+        out_specs=pl.BlockSpec(memory_space=pl.ANY),
+        scratch_shapes=[pltpu.SemaphoreType.DMA((PARTS,))],
+        compiler_params=pltpu.CompilerParams(vmem_limit_bytes=62 * 2**20),
+        name="hand_over",
+    )(made)
 
 
 def solution(mesh):

time: 28.5 us -> 43.6 us (1.53)
  Pallas kernels: 26.4 us -> 43.4 us
  local copies, waits for them, and re-layouts: 1.87 us -> 0 us
    pallas_call x0 -> x1, Pallas kernels: none -> 17 us  [per_device(): pl.pallas_call(hand_over, out_shape=jax.ShapeDtypeStruct((512, 256), jnp....]
    unnamed x1 -> x0, local copies, waits for them, and re-layouts: 1.87 us -> none
where the time goes in v5:
time: 43.6 us; the launch traced here: 43.4 us
  Pallas kernels  43.4 us (100%)
    pallas_call x1, Pallas kernels, per_device(): pl.pallas_call(kernel, out_shape=jax.ShapeDtypeStruct((512, 256), jnp.flo...  26.4 us
    pallas_call x1, Pallas kernels, per_device(): pl.pallas_call(hand_over, out_shape=jax.ShapeDtypeStruct((512, 256), jnp....  17 us

profile of v5, /device:TPU:257, one launch (start us, length us, event | category | flops | bytes accessed | tf_op | source)
XLA Modules:
  0.0 43.4 jit_solution(3265280140675837657)
XLA Ops:
  0.0 26.4 %block_product.1.made = f32[512,256]{1,0:T(8,128)} custom-call(bf16[1,1,2,128,128]{4,3,2,1,0:T(8,128)(2,1)} %s_hbm.1, s32[1,1,2]{2,1,0:T(1,128)} %ss_hbm.1, bf16[4,1,1,1,128,128]{5,4,3,2,1,0:T(8,128)(2,1)} %x_hbm.1, s32[1,1,1,4]{3,2,1,0:T(1,128)} %bitcast.1), custom_call_target="tpu_custom_call" | custom-call | flops 1073741824 | bytes 1048576 | tf_op jit(solution)/shard_map/block_product/pallas_call | solution.py:266
  26.4 17.0 %hand_over.1 = f32[512,256]{1,0:T(8,128)} custom-call(f32[512,256]{1,0:T(8,128)} %block_product.1.made), custom_call_target="tpu_custom_call" | custom-call | tf_op jit(solution)/shard_map/hand_over/pallas_call | solution.py:295

commit v6 on v4

--- a/solution.py
+++ b/solution.py
@@ -23,7 +23,10 @@
     ("r", (4, 5, 6, 7,)),
     ("z", (4, 5, 6, 7,)),
     ("d", (3, 5, 4,)),
-    ("s", (0, 1, 2, 3, 4, 5, 6, 7,)),
+    ("s", (0, 1, 2, 3, 4, 5, 6,)),
+    ("p", (0, 1, 2, 3, 4,)),
+    ("s", (7,)),
+    ("p", (5, 6, 7,)),
 )
 HIGH = (
     ("y", (1, 7, 2, 6,)),
@@ -32,7 +35,10 @@
     ("d", (1, 7, 2, 6,)),
     ("z", (0, 1, 2, 3,)),
     ("d", (3, 5, 4,)),
-    ("s", (4, 5, 6, 7, 0, 1, 2, 3,)),
+    ("s", (4, 5, 6, 7, 0, 1, 2,)),
+    ("p", (4, 5, 6, 7,)),
+    ("s", (3,)),
+    ("p", (0, 1, 2, 3,)),
 )
 
 
@@ -145,7 +151,7 @@
         block = xbuf.at[pl.ds((l * NY + origin) * 2, 2)]
         remote(block, block, send.at[5], sib_x, sibling)
 
-    def group(zs):
+    def group(zs, first):
         x_tiles, targets, blocks = [], [], []
         for c in range(NX):
             r = (zs % 2) * 4 + c
@@ -169,14 +175,16 @@
                 ]
                 row.append((blocks[c][0] * hit[0] + blocks[c][1] * hit[1]).reshape(B, B))
             part = jnp.dot(jnp.concatenate(row, axis=1), x_tile, preferred_element_type=jnp.float32)
-            if zs == 0:
+            if first:
                 out[pl.ds(br * B, B), :] = part
             else:
                 out[pl.ds(br * B, B), :] += part
 
-    def product(zs):
+    def product(zs, first):
+        if first:
+            wait_bytes(xbuf.at[pl.ds(0, 16)], sib_x)
         wait_bytes(sbuf.at[pl.ds(0, NX)], sib_s.at[zs])
-        group(zs)
+        group(zs, first)
 
     def share_s(zs):
         wait_bytes(rows(198), x_sem.at[zs])
@@ -204,7 +212,7 @@
             pl.semaphore_wait(y_ready.at[Y_STEPS.index(step)], 1)
         send_y(0, step)
 
-    def run(order):
+    def run(order, first):
         for kind, k in [(kind, k) for kind, ks in order for k in ks]:
             if kind == "y":
                 own_y(k)
@@ -216,6 +224,8 @@
                 pass_x(k)
             elif kind == "d":
                 pass_y(k)
+            elif kind == "p":
+                product(k, k == first)
             else:
                 share_s(k)
 
@@ -230,15 +240,12 @@
 
     @pl.when(z < NZ // 2)
     def _():
-        run(LOW)
+        run(LOW, 0)
 
     @pl.when(z >= NZ // 2)
     def _():
-        run(HIGH)
-
-    wait_bytes(xbuf.at[pl.ds(0, 16)], sib_x)
-    for zs in range(NZ):
-        product(zs)
+        run(HIGH, 4)
+
     wait_bytes(sbuf.at[pl.ds(0, 31)], send.at[0])
     wait_bytes(sl.at[pl.ds(0, 62)], send.at[1])
     wait_bytes(sbuf.at[pl.ds(0, 32)], send.at[2])

time: 28.5 us -> 28 us (0.982)
  the two profiles are of different devices: /device:TPU:257 before, /device:TPU:89 now
where the time goes in v6:
time: 28 us; the launch traced here: 27.8 us
  Pallas kernels  25.9 us (92%)
  local copies, waits for them, and re-layouts  1.87 us (7%)
    pallas_call x1, Pallas kernels, per_device(): pl.pallas_call(kernel, out_shape=jax.ShapeDtypeStruct((512, 256), jnp.flo...  25.9 us
    unnamed x1, local copies, waits for them, and re-layouts  1.87 us

profile of v6, /device:TPU:89, one launch (start us, length us, event | category | flops | bytes accessed | tf_op | source)
XLA Modules:
  0.0 27.8 jit_solution(14564499646493930790)
XLA Ops:
  0.0 25.9 %block_product.1 = f32[512,256]{1,0:T(8,128)} custom-call(bf16[1,1,2,128,128]{4,3,2,1,0:T(8,128)(2,1)} %s_hbm.1, s32[1,1,2]{2,1,0:T(1,128)} %ss_hbm.1, bf16[4,1,1,1,128,128]{5,4,3,2,1,0:T(8,128)(2,1)} %x_hbm.1, s32[1,1,1,4]{3,2,1,0:T(1,128)} %bitcast.1), custom_call_target="tpu_custom_call" | custom-call | flops 1073741824 | bytes 1048576 | tf_op jit(solution)/shard_map/block_product/pallas_call | solution.py:258
  25.9 1.9 %copy.6 = f32[512,256]{1,0:T(8,128)} copy(f32[512,256]{1,0:T(8,128)} %block_product.1) | data formatting | bytes 1048576

commit v7 on v6

--- a/solution.py
+++ b/solution.py
@@ -42,7 +42,7 @@
 )
 
 
-def kernel(s_hbm, ss_hbm, x_hbm, xs_hbm, out, sbuf, xbuf, sl, xl, dummy, ssm, xsm,
+def kernel(s_hbm, ss_hbm, x_hbm, xs_hbm, out, total, sbuf, xbuf, sl, xl, dummy, ssm, xsm,
            z_sem, x_sem, y_sem, sib_s, sib_x, send, local, ready, y_ready):
     y = lax.axis_index("row")
     col = lax.axis_index("col")
@@ -151,7 +151,7 @@
         block = xbuf.at[pl.ds((l * NY + origin) * 2, 2)]
         remote(block, block, send.at[5], sib_x, sibling)
 
-    def group(zs, first):
+    def group(zs, first, last):
         x_tiles, targets, blocks = [], [], []
         for c in range(NX):
             r = (zs % 2) * 4 + c
@@ -176,15 +176,21 @@
                 row.append((blocks[c][0] * hit[0] + blocks[c][1] * hit[1]).reshape(B, B))
             part = jnp.dot(jnp.concatenate(row, axis=1), x_tile, preferred_element_type=jnp.float32)
             if first:
-                out[pl.ds(br * B, B), :] = part
+                total[pl.ds(br * B, B), :] = part
             else:
-                out[pl.ds(br * B, B), :] += part
-
-    def product(zs, first):
+                total[pl.ds(br * B, B), :] += part
+            if last:
+                finished(br).start()
+
+    def finished(br):
+        block = pl.ds(br * B, B)
+        return pltpu.make_async_copy(total.at[block], out.at[block], local.at[4 + br])
+
+    def product(zs, first, last):
         if first:
             wait_bytes(xbuf.at[pl.ds(0, 16)], sib_x)
         wait_bytes(sbuf.at[pl.ds(0, NX)], sib_s.at[zs])
-        group(zs, first)
+        group(zs, first, last)
 
     def share_s(zs):
         wait_bytes(rows(198), x_sem.at[zs])
@@ -212,7 +218,7 @@
             pl.semaphore_wait(y_ready.at[Y_STEPS.index(step)], 1)
         send_y(0, step)
 
-    def run(order, first):
+    def run(order, first, last):
         for kind, k in [(kind, k) for kind, ks in order for k in ks]:
             if kind == "y":
                 own_y(k)
@@ -225,7 +231,7 @@
             elif kind == "d":
                 pass_y(k)
             elif kind == "p":
-                product(k, k == first)
+                product(k, k == first, k == last)
             else:
                 share_s(k)
 
@@ -240,11 +246,11 @@
 
     @pl.when(z < NZ // 2)
     def _():
-        run(LOW, 0)
+        run(LOW, 0, 7)
 
     @pl.when(z >= NZ // 2)
     def _():
-        run(HIGH, 4)
+        run(HIGH, 4, 3)
 
     wait_bytes(sbuf.at[pl.ds(0, 31)], send.at[0])
     wait_bytes(sl.at[pl.ds(0, 62)], send.at[1])
@@ -252,6 +258,8 @@
     wait_bytes(xbuf.at[pl.ds(0, 14)], send.at[3])
     wait_bytes(xl.at[pl.ds(0, 28)], send.at[4])
     wait_bytes(xbuf.at[pl.ds(0, 16)], send.at[5])
+    for br in range(4):
+        finished(br).wait()
 
 
 def per_device(s_values, s_slots, x_values, x_slots):
@@ -259,8 +267,9 @@
         kernel,
         out_shape=jax.ShapeDtypeStruct((512, 256), jnp.float32),
         in_specs=[pl.BlockSpec(memory_space=pl.ANY)] * 4,
-        out_specs=pl.BlockSpec(memory_space=pltpu.VMEM),
+        out_specs=pl.BlockSpec(memory_space=pl.ANY),
         scratch_shapes=[
+            pltpu.VMEM((512, 256), jnp.float32),
             pltpu.VMEM((64, B, B), jnp.bfloat16),
             pltpu.VMEM((32, B, B), jnp.bfloat16),
             pltpu.VMEM((64, 1, B), jnp.int32),
@@ -274,7 +283,7 @@
             pltpu.SemaphoreType.DMA((8,)),
             pltpu.SemaphoreType.DMA,
             pltpu.SemaphoreType.DMA((6,)),
-            pltpu.SemaphoreType.DMA((4,)),
+            pltpu.SemaphoreType.DMA((8,)),
             pltpu.SemaphoreType.REGULAR((8,)),
             pltpu.SemaphoreType.REGULAR((4,)),
         ],

time: 28 us -> 27.9 us (level)
  no operation moved by 1% of the time
where the time goes in v7:
time: 27.9 us; the launch traced here: 27.7 us
  Pallas kernels  25.8 us (92%)
  local copies, waits for them, and re-layouts  1.87 us (7%)
    pallas_call x1, Pallas kernels, per_device(): pl.pallas_call(kernel, out_shape=jax.ShapeDtypeStruct((512, 256), jnp.flo...  25.8 us
    unnamed x1, local copies, waits for them, and re-layouts  1.87 us

profile of v7, /device:TPU:89, one launch (start us, length us, event | category | flops | bytes accessed | tf_op | source)
XLA Modules:
  0.0 27.7 jit_solution(11058319261369240653)
XLA Ops:
  0.0 25.8 %block_product.1 = f32[512,256]{1,0:T(8,128)} custom-call(bf16[1,1,2,128,128]{4,3,2,1,0:T(8,128)(2,1)} %s_hbm.1, s32[1,1,2]{2,1,0:T(1,128)} %ss_hbm.1, bf16[4,1,1,1,128,128]{5,4,3,2,1,0:T(8,128)(2,1)} %x_hbm.1, s32[1,1,1,4]{3,2,1,0:T(1,128)} %bitcast.1), custom_call_target="tpu_custom_call" | custom-call | flops 1073741824 | bytes 1048576 | tf_op jit(solution)/shard_map/block_product/pallas_call | solution.py:266
  25.8 1.9 %copy.6 = f32[512,256]{1,0:T(8,128)} copy(f32[512,256]{1,0:T(8,128)} %block_product.1) | data formatting | bytes 1048576

commit v8 on v6

--- a/solution.py
+++ b/solution.py
@@ -24,9 +24,9 @@
     ("z", (4, 5, 6, 7,)),
     ("d", (3, 5, 4,)),
     ("s", (0, 1, 2, 3, 4, 5, 6,)),
-    ("p", (0, 1, 2, 3, 4,)),
+    ("p", (0, 1, 2, 3, 4, 5,)),
     ("s", (7,)),
-    ("p", (5, 6, 7,)),
+    ("p", (6, 7,)),
 )
 HIGH = (
     ("y", (1, 7, 2, 6,)),
@@ -36,9 +36,9 @@
     ("z", (0, 1, 2, 3,)),
     ("d", (3, 5, 4,)),
     ("s", (4, 5, 6, 7, 0, 1, 2,)),
-    ("p", (4, 5, 6, 7,)),
+    ("p", (4, 5, 6, 7, 0, 1,)),
     ("s", (3,)),
-    ("p", (0, 1, 2, 3,)),
+    ("p", (2, 3,)),
 )
 
 

time: 28 us -> 28.2 us (level)
  the two profiles are of different devices: /device:TPU:89 before, /device:TPU:257 now
where the time goes in v8:
time: 28.2 us; the launch traced here: 28 us
  Pallas kernels  26.1 us (93%)
  local copies, waits for them, and re-layouts  1.87 us (7%)
    pallas_call x1, Pallas kernels, per_device(): pl.pallas_call(kernel, out_shape=jax.ShapeDtypeStruct((512, 256), jnp.flo...  26.1 us
    unnamed x1, local copies, waits for them, and re-layouts  1.87 us

profile of v8, /device:TPU:257, one launch (start us, length us, event | category | flops | bytes accessed | tf_op | source)
XLA Modules:
  0.0 28.0 jit_solution(17572862255529797074)
XLA Ops:
  0.0 26.1 %block_product.1 = f32[512,256]{1,0:T(8,128)} custom-call(bf16[1,1,2,128,128]{4,3,2,1,0:T(8,128)(2,1)} %s_hbm.1, s32[1,1,2]{2,1,0:T(1,128)} %ss_hbm.1, bf16[4,1,1,1,128,128]{5,4,3,2,1,0:T(8,128)(2,1)} %x_hbm.1, s32[1,1,1,4]{3,2,1,0:T(1,128)} %bitcast.1), custom_call_target="tpu_custom_call" | custom-call | flops 1073741824 | bytes 1048576 | tf_op jit(solution)/shard_map/block_product/pallas_call | solution.py:258
  26.1 1.9 %copy.6 = f32[512,256]{1,0:T(8,128)} copy(f32[512,256]{1,0:T(8,128)} %block_product.1) | data formatting | bytes 1048576
